TPU v7x, 32 devices: a whole 2x2x4 slice. The times are simulated.
32 devices in a mesh: head: 4 (over y, core), tok: 8 (over z, x).
Axes of the slice: x: 2, y: 2, z: 4, core: 2. Of those that a mesh axis runs over, the one named last changes fastest.
Arguments:
- queries: bfloat16 [8192, 4096], P('tok', 'head'), may hold values from -100 to 100
- keys: bfloat16 [8192, 4096], P('tok', 'head'), may hold values from -6 to 6
- values: bfloat16 [8192, 4096], P('tok', 'head'), may hold values from -6 to 6
- step_size: float32 [8192, 8], P('tok', 'head'), may hold values from 0.00012207031 to 0.0012207031
- fast_one: bfloat16 [8, 512, 512], P('head'), may hold values from -0.25 to 0.25
- fast_three: bfloat16 [8, 512, 512], P('head'), may hold values from -0.25 to 0.25
- fast_two: bfloat16 [8, 512, 512], P('head'), may hold values from -0.25 to 0.25
- out_proj: bfloat16 [4096, 4096], P('tok', 'head'), may hold values from -0.09375 to 0.09375
- view_units: int32 [16], replicated, may hold values from 1 to 8, 64 in all
- evening: int32 [8, 8], P('tok'), may hold values from 0 to 7, each once within a row
Outputs:
- evened: bfloat16 [8192, 4096], P('tok', 'head')
Inputs may be any that keep to these rules, and one draw needn't show every extreme that they name: `view_units`: the lengths sum to 64; the longest is exactly 8. `evening`: each row is a permutation of the token shards.
All inputs are finite; a program needn't handle non-finite values.
Results may differ from a plain program's by a relative error of at most 0.01.
The roundings to bfloat16 on the way count: a program that leaves them out, or rounds other values in their place, can miss the bound.
Values may be sent and summed in bfloat16 or wider, within the bound.
A program may use at most 128 MiB of HBM per device.

v0:
```python
import jax
import jax.numpy as jnp
from jax import lax
from jax.sharding import PartitionSpec as P

DH = 512
VIEW_UNIT = 128
VIEW_MOST = 8


def from_behind(value, axis, steps):
    count = lax.axis_size(axis)
    leading, last = (max(0, -steps), min(count, count - steps))
    return lax.ppermute(value, axis, [(source, source + steps) for source in range(leading, last)])


def view_lookup(view_units, positions, total_tokens):
    view_ends = jnp.cumsum(view_units) * VIEW_UNIT
    inside = (positions >= 0) & (positions < total_tokens)
    labels = jnp.sum((positions[:, None] >= view_ends[None, :]).astype(jnp.int32), axis=1)
    return jnp.where(inside, labels, -1)


def rms_rows(rows):
    return rows * lax.rsqrt(jnp.mean(rows * rows, axis=-1, keepdims=True) + 1e-06)


def local(
    queries, keys, values, step_size, fast_one, fast_three, fast_two, out_proj, view_units, evening
):
    shard_count = lax.axis_size("tok")
    my_shard = lax.axis_index("tok")
    tok_dev = queries.shape[0]
    local_width = queries.shape[1]
    heads_here = local_width // DH
    total_tokens = tok_dev * shard_count
    reach_span = (VIEW_MOST * VIEW_UNIT + tok_dev - 2) // tok_dev
    scale = DH ** (-0.5)
    local_rows = jnp.arange(tok_dev, dtype=jnp.int32)
    stacked = jnp.stack([keys, values])
    pieces = []
    labels = []
    offsets = list(range(reach_span, 0, -1)) + [0] + list(range(-1, -reach_span - 1, -1))
    for offset in offsets:
        if offset == 0:
            pieces.append(stacked)
        else:
            pieces.append(from_behind(stacked, "tok", offset))
        labels.append(
            view_lookup(view_units, (my_shard - offset) * tok_dev + local_rows, total_tokens)
        )
    window = jnp.concatenate(pieces, axis=1)
    key_views = jnp.concatenate(labels)
    key_heads = window[0].reshape(-1, heads_here, DH)
    value_heads = window[1].reshape(-1, heads_here, DH)
    window_rows = key_heads.shape[0]
    query_views = view_lookup(view_units, my_shard * tok_dev + local_rows, total_tokens)
    block_rows = min(512, tok_dev)
    n_blocks = tok_dev // block_rows
    key_span = min(window_rows, block_rows + 2 * VIEW_MOST * VIEW_UNIT)
    lead_shift = reach_span * tok_dev - VIEW_MOST * VIEW_UNIT

    def attend(block_index):
        start = block_index * block_rows
        key_start = jnp.clip(start + lead_shift, 0, window_rows - key_span)
        query_rows = lax.dynamic_slice_in_dim(queries, start, block_rows, 0).reshape(
            block_rows, heads_here, DH
        )
        row_views = lax.dynamic_slice_in_dim(query_views, start, block_rows, 0)
        near_keys = lax.dynamic_slice_in_dim(key_heads, key_start, key_span, 0)
        near_values = lax.dynamic_slice_in_dim(value_heads, key_start, key_span, 0)
        near_views = lax.dynamic_slice_in_dim(key_views, key_start, key_span, 0)
        scores = (
            jnp.einsum("qhd,khd->hqk", query_rows, near_keys, preferred_element_type=jnp.float32)
            * scale
        )
        same_view = row_views[:, None] == near_views[None, :]
        scores = jnp.where(same_view[None], scores, -1e30)
        top = jnp.max(scores, axis=-1, keepdims=True)
        weights = jnp.exp(scores - top)
        probs = (weights / jnp.sum(weights, axis=-1, keepdims=True)).astype(jnp.bfloat16)
        out_rows = jnp.einsum(
            "hqk,khd->qhd", probs, near_values, preferred_element_type=jnp.float32
        )
        return out_rows.reshape(block_rows, local_width)

    attended = lax.map(attend, jnp.arange(n_blocks, dtype=jnp.int32)).reshape(tok_dev, local_width)
    query_norm = rms_rows(queries.reshape(tok_dev, heads_here, DH).astype(jnp.float32)).astype(
        jnp.bfloat16
    )
    key_norm = rms_rows(keys.reshape(tok_dev, heads_here, DH).astype(jnp.float32)).astype(
        jnp.bfloat16
    )
    gate_pre = jnp.einsum("thd,hdf->htf", key_norm, fast_one, preferred_element_type=jnp.float32)
    up_pre = jnp.einsum("thd,hdf->htf", key_norm, fast_three, preferred_element_type=jnp.float32)
    gate_sig = jax.nn.sigmoid(gate_pre)
    hidden_keys = (gate_pre * gate_sig * up_pre).astype(jnp.bfloat16)
    descent = (
        -step_size[:, :, None] * values.reshape(tok_dev, heads_here, DH).astype(jnp.float32)
    ).astype(jnp.bfloat16)
    grad_two = jnp.einsum("htf,thd->hfd", hidden_keys, descent, preferred_element_type=jnp.float32)
    back = jnp.einsum("thd,hfd->htf", descent, fast_two, preferred_element_type=jnp.float32)
    grad_gate = (back * up_pre * gate_sig * (1.0 + gate_pre * (1.0 - gate_sig))).astype(
        jnp.bfloat16
    )
    grad_up = (back * gate_pre * gate_sig).astype(jnp.bfloat16)
    grad_one = jnp.einsum("thd,htf->hdf", key_norm, grad_gate, preferred_element_type=jnp.float32)
    grad_three = jnp.einsum("thd,htf->hdf", key_norm, grad_up, preferred_element_type=jnp.float32)
    total_one, total_three, total_two = lax.psum((grad_one, grad_three, grad_two), "tok")
    new_one = (fast_one.astype(jnp.float32) - total_one).astype(jnp.bfloat16)
    new_three = (fast_three.astype(jnp.float32) - total_three).astype(jnp.bfloat16)
    new_two = (fast_two.astype(jnp.float32) - total_two).astype(jnp.bfloat16)
    gate_q = jnp.einsum("thd,hdf->htf", query_norm, new_one, preferred_element_type=jnp.float32)
    up_q = jnp.einsum("thd,hdf->htf", query_norm, new_three, preferred_element_type=jnp.float32)
    hidden_q = (gate_q * jax.nn.sigmoid(gate_q) * up_q).astype(jnp.bfloat16)
    fast_out = jnp.einsum(
        "htf,hfd->thd", hidden_q, new_two, preferred_element_type=jnp.float32
    ).reshape(tok_dev, local_width)
    mixed = (attended + fast_out).astype(jnp.bfloat16)
    mixed_full = lax.all_gather(mixed, "head", axis=1, tiled=True)
    projected = jnp.dot(
        mixed_full,
        lax.all_gather(out_proj, "tok", axis=0, tiled=True),
        preferred_element_type=jnp.float32,
    ).astype(jnp.bfloat16)
    tiles = projected.reshape(shard_count, tok_dev // shard_count, out_proj.shape[1])
    targets = evening.reshape(shard_count)
    match = (targets[None, :] == jnp.arange(shard_count, dtype=jnp.int32)[:, None]).astype(
        jnp.int32
    )
    order_index = jnp.argmax(match, axis=1)
    outgoing = tiles[order_index]
    arrived = lax.all_to_all(outgoing, "tok", split_axis=0, concat_axis=0, tiled=True)
    return arrived.reshape(tok_dev, out_proj.shape[1])


def solution(mesh):
    return jax.shard_map(
        local,
        mesh=mesh,
        in_specs=(
            P("tok", "head"),
            P("tok", "head"),
            P("tok", "head"),
            P("tok", "head"),
            P("head", None, None),
            P("head", None, None),
            P("head", None, None),
            P("tok", "head"),
            P(),
            P("tok", None),
        ),
        out_specs=P("tok", "head"),
        check_vma=False,
    )
```

profile of v0, /device:TPU:0, one launch (start us, length us, event | category | flops | bytes accessed | tf_op | source)
XLA Modules:
  0.0 614.9 jit_solution(3195934623756966856)
XLA Ops:
  9.9 3.1 copy.90
  24.1 3.6 fusion.25
  30.7 3.9 copy.82
  34.7 4.0 pad_maximum_fusion.1
  38.7 6.9 %collective-permute-start = (bf16[2,1024,1024]{1,2,0:T(8,128)(2,1)}, bf16[2,1024,1024]{1,2,0:T(8,128)(2,1)}, u32[]{:S(2)}, u32[]{:S(2)}) collective-permute-start(bf16[2,1024,1024]{1,2,0:T(8,128)(2,1)} %pad_maximum_fusion.1), channel_id=1, source_target_pairs={{0,1},{1,2},{2,3},{3,4},{4,5},{5,6},{6,7},{8,9},{9,10},{10,11},{11... | collective-permute-start | bytes 12582920 | tf_op jit(solution)/shard_map/ppermute | solution.py:14
  47.1 3.9 copy.84
  51.1 4.1 copy.96
  57.6 206.4 %collective-permute-done = bf16[2,1024,1024]{1,2,0:T(8,128)(2,1)} collective-permute-done((bf16[2,1024,1024]{1,2,0:T(8,128)(2,1)}, bf16[2,1024,1024]{1,2,0:T(8,128)(2,1)}, u32[]{:S(2)}, u32[]{:S(2)}) %collective-permute-start) | collective-permute-done | bytes 4194336 | tf_op jit(solution)/shard_map/ppermute | solution.py:14
  263.9 6.0 pad_maximum_fusion
  270.0 5.2 fusion.38
  275.1 60.7 %while.10 = (s32[]{:T(128)}, f32[2,512,1024]{2,1,0:T(8,128)}, s32[2]{0:T(128)S(1)}, bf16[3072,2,512]{0,2,1:T(8,128)(2,1)}, s32[1024]{0:T(1024)S(1)}, /*index=5*/...) while((s32[]{:T(128)}, f32[2,512,1024]{2,1,0:T(8,128)}, ...), condition=%wide.region_7.8_spmd, body=%wide.region_4.7_spmd.sunk | while | flops 5385751040 | bytes 47756000 | solution.py:87
  278.8 13.4 %fusion.59 = (f32[2,512]{1,0:T(2,128)S(1)}, f32[2,512,2560]{2,1,0:T(8,128)}) fusion(pred[512,2560]{1,0:T(8,128)(4,1)S(1)} %broadcast_compare_fusion.2, bf16[512,2,512]{0,2,1:T(8,128)(2,1)S(1)} %bitcast.55, bf16[3072,2,512]{0,2,1:T(8,128)(2,1)} %get-tuple-element.204, s32[]{:T(128)S(6)} %min.5), kind=kOutput, calls=%fused_computation.67.clone.1 | convolution fusion | flops 2694842880 | bytes 18092036 | tf_op jit(solution)/shard_map/while/body/eval_jaxpr/sub | solution.py:80
  292.2 10.0 %fusion.60 = f32[2,512,512]{2,1,0:T(8,128)} fusion(bf16[3072,2,512]{0,2,1:T(8,128)(2,1)} %get-tuple-element.200, s32[]{:T(128)S(6)} %min.5, f32[2,512,2560]{2,1,0:T(8,128)} %get-tuple-element.169, f32[2,512]{1,0:T(2,128)S(1)} %get-tuple-element.170), kind=kOutput, calls=%fused_computation.10.clone.1 | convolution fusion | flops 2689597440 | bytes 17829892 | tf_op jit(solution)/shard_map/while/body/eval_jaxpr/hqk,khd->qhd/dot_general | solution.py:82
  309.3 13.1 %fusion.59 = (f32[2,512]{1,0:T(2,128)S(1)}, f32[2,512,2560]{2,1,0:T(8,128)}) fusion(pred[512,2560]{1,0:T(8,128)(4,1)S(1)} %broadcast_compare_fusion.2, bf16[512,2,512]{0,2,1:T(8,128)(2,1)S(1)} %bitcast.55, bf16[3072,2,512]{0,2,1:T(8,128)(2,1)} %get-tuple-element.204, s32[]{:T(128)S(6)} %min.5), kind=kOutput, calls=%fused_computation.67.clone.1 | convolution fusion | flops 2694842880 | bytes 18092036 | tf_op jit(solution)/shard_map/while/body/eval_jaxpr/sub | solution.py:80
  322.4 10.0 %fusion.60 = f32[2,512,512]{2,1,0:T(8,128)} fusion(bf16[3072,2,512]{0,2,1:T(8,128)(2,1)} %get-tuple-element.200, s32[]{:T(128)S(6)} %min.5, f32[2,512,2560]{2,1,0:T(8,128)} %get-tuple-element.169, f32[2,512]{1,0:T(2,128)S(1)} %get-tuple-element.170), kind=kOutput, calls=%fused_computation.10.clone.1 | convolution fusion | flops 2689597440 | bytes 17829892 | tf_op jit(solution)/shard_map/while/body/eval_jaxpr/hqk,khd->qhd/dot_general | solution.py:82
  335.8 15.9 %all-reduce.3.cloned.1.call-done = (f32[2,512,512]{2,1,0:T(8,128)}, f32[2,512,512]{2,1,0:T(8,128)}, f32[2,512,512]{2,1,0:T(8,128)}) async-done(((f32[2,512,512]{2,1,0:T(8,128)}, f32[2,512,512]{2,1,0:T(8,128)}, f32[2,512,512]{2,1,0:T(8,128)}), (f32[2,512,512]{2,1,0:T(8,128)}, f32[2,512,512]{2,1,0:T(8,128)}, f32[2,512,512]{2,1,0:T(8,128)})) %all-reduce.3.cloned.1.call-update) | async-done | bytes 6291472 | tf_op jit(solution)/shard_map/psum | solution.py:109
  351.8 6.2 %fusion.27 = f32[2,1024,512]{2,1,0:T(8,128)} fusion(f32[2,512,512]{2,1,0:T(8,128)} %get-tuple-element.109, bf16[2,512,512]{2,1,0:T(8,128)(2,1)S(1)} %copy-done.2, f32[1024,2,512]{2,0,1:T(8,128)} %copy.96, f32[1024,2]{0,1:T(2,128)S(1)} %add_rsqrt_fusion), kind=kOutput, calls=%fused_computation.44 | convolution fusion | flops 1077411840 | bytes 11542528 | tf_op jit(solution)/shard_map/thd,hdf->htf/dot_general | solution.py:113
  358.0 10.4 %fusion.26 = f32[2,512,1024]{2,1,0:T(8,128)} fusion(f32[2,1024,512]{2,1,0:T(8,128)} %fusion.27, f32[2,512,512]{2,1,0:T(8,128)} %get-tuple-element.110, bf16[2,512,512]{2,1,0:T(8,128)(2,1)S(1)} %copy-done.6, f32[2,512,512]{2,1,0:T(8,128)} %get-tuple-element.111, bf16[2,512,512]{2,1,0:T(8,128)(2,1)S(1)} %copy-done.4, f32[1024,2,512]{2,0,1:T(8,128)} %copy.96, ...), kind=kOutput, calls=%fused_computation.43 | convolution fusion | flops 2159017984 | bytes 18882560 | tf_op jit(solution)/shard_map/htf,hfd->thd/dot_general | solution.py:116
  368.4 5.4 copy.100
  373.8 5.6 fusion.22
  380.0 98.0 %all-gather.5.cloned.1.call-done = bf16[4096,1024]{1,0:T(8,128)(2,1)} async-done(((bf16[512,1024]{1,0:T(8,128)(2,1)}), bf16[4096,1024]{1,0:T(8,128)(2,1)}) %all-gather.5.cloned.1.call-update) | async-done | bytes 8388624 | tf_op jit(solution)/shard_map/all_gather | solution.py:123
  478.1 58.2 %all-gather.3.cloned.1.call-done = bf16[1024,4096]{1,0:T(8,128)(2,1)} async-done(((bf16[1024,1024]{1,0:T(8,128)(2,1)}), bf16[1024,4096]{1,0:T(8,128)(2,1)}) %all-gather.3.cloned.1.call-update) | async-done | bytes 8388624 | tf_op jit(solution)/shard_map/all_gather | solution.py:120
  536.2 14.6 %convolution_convert_fusion = bf16[1024,1024]{1,0:T(8,128)(2,1)} fusion(bf16[1024,4096]{1,0:T(8,128)(2,1)} %all-gather.3.cloned.1.call-done, bf16[4096,1024]{1,0:T(8,128)(2,1)} %all-gather.5.cloned.1.call-done), kind=kOutput, calls=%fused_computation.42 | convolution fusion | flops 8590983168 | bytes 18874368 | tf_op jit(solution)/shard_map/dot_general | solution.py:121
  553.1 53.9 %all_to_all.5 = bf16[8,128,1024]{2,1,0:T(8,128)(2,1)S(1)} all-to-all(bf16[8,128,1024]{2,1,0:T(8,128)(2,1)S(1)} %gather_fusion), channel_id=1, replica_groups=mesh['head'=4,'tok'=8] {'tok'}, dimensions={0} | all-to-all | bytes 4194304 | tf_op jit(solution)/shard_map/all_to_all | solution.py:133
  (72 shorter events, 38.2 us)
Async XLA Ops:
  6.5 345.2 %all-reduce.3.cloned.1.call-start = ((), (), s32[]{:S(2)}) async-start(), calls=%async_computation.3 | async-start | bytes 12582912 | tf_op jit(solution)/shard_map/psum | solution.py:109
  12.9 2.6 copy-start.1
  15.6 1.3 copy-start.3
  16.9 1.6 copy-start
  18.5 0.7 copy-start.7
  18.5 1.2 copy-start.5
  30.7 447.4 %all-gather.5.cloned.1.call-start = ((), (), s32[]{:S(2)}) async-start(), calls=%async_computation.2 | async-start | bytes 9437184 | tf_op jit(solution)/shard_map/all_gather | solution.py:123
  34.7 12.3 %copy-start.8 = (s32[16]{0:T(128)S(1)}, s32[16]{0:T(128)}, u32[]{:S(2)}) copy-start(s32[16]{0:T(128)} %param.20) | copy-start | bytes 196
  38.7 225.3 %collective-permute-start = (bf16[2,1024,1024]{1,2,0:T(8,128)(2,1)}, bf16[2,1024,1024]{1,2,0:T(8,128)(2,1)}, u32[]{:S(2)}, u32[]{:S(2)}) collective-permute-start(bf16[2,1024,1024]{1,2,0:T(8,128)(2,1)} %pad_maximum_fusion.1), channel_id=1, source_target_pairs={{0,1},{1,2},{2,3},{3,4},{4,5},{5,6},{6,7},{8,9},{9,10},{10,11},{11... | collective-permute-start | bytes 12582920 | tf_op jit(solution)/shard_map/ppermute | solution.py:14
  45.6 218.3 %collective-permute-start.1 = (bf16[2,1024,1024]{1,2,0:T(8,128)(2,1)}, bf16[2,1024,1024]{1,2,0:T(8,128)(2,1)}, u32[]{:S(2)}, u32[]{:S(2)}) collective-permute-start(bf16[2,1024,1024]{1,2,0:T(8,128)(2,1)} %pad_maximum_fusion.1), channel_id=1, source_target_pairs={{1,0},{2,1},{3,2},{4,3},{5,4},{6,5},{7,6},{9,8},{10,9},{11,10},{12... | collective-permute-start | bytes 12582920 | tf_op jit(solution)/shard_map/ppermute | solution.py:14
  46.9 489.3 %all-gather.3.cloned.1.call-start = ((), (), s32[]{:S(2)}) async-start(), calls=%async_computation.1 | async-start | bytes 10485760 | tf_op jit(solution)/shard_map/all_gather | solution.py:120
  275.1 76.6 %copy-start.2 = (bf16[2,512,512]{2,1,0:T(8,128)(2,1)S(1)}, bf16[2,512,512]{2,1,0:T(8,128)(2,1)}, u32[]{:S(2)}) copy-start(bf16[2,512,512]{2,1,0:T(8,128)(2,1)} %param.16) | copy-start | bytes 3145732
  351.8 6.2 %copy-start.4 = (bf16[2,512,512]{2,1,0:T(8,128)(2,1)S(1)}, bf16[2,512,512]{2,1,0:T(8,128)(2,1)}, u32[]{:S(2)}) copy-start(bf16[2,512,512]{2,1,0:T(8,128)(2,1)} %param.17) | copy-start | bytes 3145732
  351.8 6.2 %copy-start.6 = (bf16[2,512,512]{2,1,0:T(8,128)(2,1)S(1)}, bf16[2,512,512]{2,1,0:T(8,128)(2,1)}, u32[]{:S(2)}) copy-start(bf16[2,512,512]{2,1,0:T(8,128)(2,1)} %param.18) | copy-start | bytes 3145732
  373.8 5.6 copy-start.9
Sparse Core Ops, SparseCore 0:
  30.8 320.9 all-reduce.2
  354.1 123.8 all-gather.4
  479.7 56.4 all-gather.2
where the time goes:
time: 616 us; the launch traced here: 615 us
  waiting for transfers between devices  379 us (62%)
  matrix products  91.2 us (15%)
  blocking collectives  53.9 us (9%)
  local copies, waits for them, and re-layouts  44.4 us (7%)
  other arithmetic  23.7 us (4%)
  between operations  13.3 us (2%)
  starting transfers between devices  8.29 us (1%)
    ppermute x2, waiting for transfers between devices, from_behind(): lax.ppermute(value, axis, [(source, source + steps) for source in range(l...  206 us
    all_gather x1, waiting for transfers between devices, local(): lax.all_gather(out_proj, 'tok', axis=0, tiled=True)  98 us
    all_gather x1, waiting for transfers between devices, local(): mixed_full = lax.all_gather(mixed, 'head', axis=1, tiled=True)  58.2 us
    all_to_all x1, blocking collectives, local(): lax.all_to_all(outgoing, 'tok', split_axis=0, concat_axis=0, tiled=True)  53.9 us
    sub x2, matrix products, attend(): weights = jnp.exp(scores - top)  26.5 us
    dot_general x2, matrix products, attend(): jnp.einsum('hqk,khd->qhd', probs, near_values, preferred_element_type=jnp...  20 us
    psum x1, waiting for transfers between devices, local(): lax.psum((grad_one, grad_three, grad_two), 'tok')  15.9 us
    dot_general x1, matrix products, local(): jnp.dot(mixed_full, lax.all_gather(out_proj, 'tok', axis=0, tiled=True),...  14.6 us
  transfers between devices with their start and end apart: 5, of which 4 were waited for; matrix products, arithmetic and copies ran while one was open for 19% of the time, Pallas kernels for 0%

commit v1 on v0

v1 whole, which is shorter than its diff:
```python
import jax
import jax.numpy as jnp
from jax import lax
from jax.experimental import pallas as pl
from jax.experimental.pallas import tpu as pltpu
from jax.sharding import PartitionSpec as P

DH = 512
VIEW_UNIT = 128
VIEW_MOST = 8


def from_behind(value, axis, steps):
    count = lax.axis_size(axis)
    leading, last = (max(0, -steps), min(count, count - steps))
    return lax.ppermute(value, axis, [(source, source + steps) for source in range(leading, last)])


def rms_rows(rows):
    return rows * lax.rsqrt(jnp.mean(rows * rows, axis=-1, keepdims=True) + 1e-06)


def attend_kernel(
    first_ref, last_ref, q_ref, kp_ref, ko_ref, kn_ref, vp_ref, vo_ref, vn_ref, o_ref, k_win, v_win
):
    halo, own = kp_ref.shape[0], ko_ref.shape[0]
    unit = pl.program_id(1)

    @pl.when(unit == 0)
    def _():
        k_win[:halo, :] = kp_ref[...]
        k_win[halo : halo + own, :] = ko_ref[...]
        k_win[halo + own :, :] = kn_ref[...]
        v_win[:halo, :] = vp_ref[...]
        v_win[halo : halo + own, :] = vo_ref[...]
        v_win[halo + own :, :] = vn_ref[...]

    span = VIEW_MOST * VIEW_UNIT
    first, last = first_ref[unit], last_ref[unit]
    base = jnp.clip(first, 0, k_win.shape[0] // VIEW_UNIT - VIEW_MOST)
    rows = pl.ds(pl.multiple_of(base * VIEW_UNIT, VIEW_UNIT), span)
    scores = lax.dot_general(
        q_ref[...], k_win[rows, :], (((1,), (1,)), ((), ())), preferred_element_type=jnp.float32
    ) * (DH ** (-0.5))
    column = lax.broadcasted_iota(jnp.int32, scores.shape, 1) + base * VIEW_UNIT
    inside = (column >= first * VIEW_UNIT) & (column < last * VIEW_UNIT)
    scores = jnp.where(inside, scores, -1e30)
    top = jnp.max(scores, axis=-1, keepdims=True)
    weights = jnp.exp(scores - top)
    probs = (weights / jnp.sum(weights, axis=-1, keepdims=True)).astype(jnp.bfloat16)
    o_ref[...] = jnp.dot(probs, v_win[rows, :], preferred_element_type=jnp.float32)


def attention(first, last, queries, k_prev, keys, k_next, v_prev, values, v_next):
    own, width = queries.shape
    halo = k_prev.shape[0]
    heads = width // DH
    part = lambda rows: pl.BlockSpec((rows, DH), lambda h, u, *_: (0, h))
    unit = pl.BlockSpec((VIEW_UNIT, DH), lambda h, u, *_: (u, h))
    return pl.pallas_call(
        attend_kernel,
        grid_spec=pltpu.PrefetchScalarGridSpec(
            num_scalar_prefetch=2,
            grid=(heads, own // VIEW_UNIT),
            in_specs=[unit] + [part(halo), part(own), part(halo)] * 2,
            out_specs=unit,
            scratch_shapes=[pltpu.VMEM((own + 2 * halo, DH), jnp.bfloat16)] * 2,
        ),
        out_shape=jax.ShapeDtypeStruct((own, width), jnp.float32),
        compiler_params=pltpu.CompilerParams(vmem_limit_bytes=40 * 1024 * 1024),
        cost_estimate=pl.CostEstimate(
            flops=4 * own * width * VIEW_MOST * VIEW_UNIT,
            bytes_accessed=8 * own * width * 2,
            transcendentals=own * heads * VIEW_MOST * VIEW_UNIT,
        ),
    )(first, last, queries, k_prev, keys, k_next, v_prev, values, v_next)


def local(
    queries, keys, values, step_size, fast_one, fast_three, fast_two, out_proj, view_units, evening
):
    shard_count = lax.axis_size("tok")
    my_shard = lax.axis_index("tok")
    tok_dev = queries.shape[0]
    local_width = queries.shape[1]
    heads_here = local_width // DH
    halo = (VIEW_MOST - 1) * VIEW_UNIT
    full_proj = lax.all_gather(out_proj, "tok", axis=0, tiled=True)
    k_prev = from_behind(keys[tok_dev - halo :], "tok", 1)
    k_next = from_behind(keys[:halo], "tok", -1)
    v_prev = from_behind(values[tok_dev - halo :], "tok", 1)
    v_next = from_behind(values[:halo], "tok", -1)
    units_here = tok_dev // VIEW_UNIT
    count = view_units.shape[0]
    before = jnp.arange(count)[:, None] > jnp.arange(count)[None, :]
    starts = jnp.sum(jnp.where(before, view_units[None, :], 0), axis=1)
    ends = starts + view_units
    here = my_shard * units_here + jnp.arange(units_here, dtype=jnp.int32)
    mine = (here[:, None] >= starts[None, :]) & (here[:, None] < ends[None, :])
    shift = halo // VIEW_UNIT - my_shard * units_here
    first = jnp.sum(jnp.where(mine, starts[None, :], 0), axis=1) + shift
    last = jnp.sum(jnp.where(mine, ends[None, :], 0), axis=1) + shift
    query_norm = rms_rows(queries.reshape(tok_dev, heads_here, DH).astype(jnp.float32)).astype(
        jnp.bfloat16
    )
    key_norm = rms_rows(keys.reshape(tok_dev, heads_here, DH).astype(jnp.float32)).astype(
        jnp.bfloat16
    )
    gate_pre = jnp.einsum("thd,hdf->htf", key_norm, fast_one, preferred_element_type=jnp.float32)
    up_pre = jnp.einsum("thd,hdf->htf", key_norm, fast_three, preferred_element_type=jnp.float32)
    gate_sig = jax.nn.sigmoid(gate_pre)
    hidden_keys = (gate_pre * gate_sig * up_pre).astype(jnp.bfloat16)
    descent = (
        -step_size[:, :, None] * values.reshape(tok_dev, heads_here, DH).astype(jnp.float32)
    ).astype(jnp.bfloat16)
    grad_two = jnp.einsum("htf,thd->hfd", hidden_keys, descent, preferred_element_type=jnp.float32)
    back = jnp.einsum("thd,hfd->htf", descent, fast_two, preferred_element_type=jnp.float32)
    grad_gate = (back * up_pre * gate_sig * (1.0 + gate_pre * (1.0 - gate_sig))).astype(
        jnp.bfloat16
    )
    grad_up = (back * gate_pre * gate_sig).astype(jnp.bfloat16)
    grad_one = jnp.einsum("thd,htf->hdf", key_norm, grad_gate, preferred_element_type=jnp.float32)
    grad_three = jnp.einsum("thd,htf->hdf", key_norm, grad_up, preferred_element_type=jnp.float32)
    grads = jnp.stack([grad_one, grad_three, grad_two]).reshape(-1, DH)
    old = jnp.stack([fast_one, fast_three, fast_two]).reshape(-1, DH)
    share = grads.shape[0] // shard_count
    total = lax.psum_scatter(grads, "tok", scatter_dimension=0, tiled=True)
    old_share = lax.dynamic_slice_in_dim(old, my_shard * share, share, 0)
    new_share = (old_share.astype(jnp.float32) - total).astype(jnp.bfloat16)
    new = lax.all_gather(new_share, "tok", axis=0, tiled=True)
    new_one, new_three, new_two = new.reshape((3,) + fast_one.shape)
    gate_q = jnp.einsum("thd,hdf->htf", query_norm, new_one, preferred_element_type=jnp.float32)
    up_q = jnp.einsum("thd,hdf->htf", query_norm, new_three, preferred_element_type=jnp.float32)
    hidden_q = (gate_q * jax.nn.sigmoid(gate_q) * up_q).astype(jnp.bfloat16)
    fast_out = jnp.einsum(
        "htf,hfd->thd", hidden_q, new_two, preferred_element_type=jnp.float32
    ).reshape(tok_dev, local_width)
    attended = attention(first, last, queries, k_prev, keys, k_next, v_prev, values, v_next)
    mixed = (attended + fast_out).astype(jnp.bfloat16)
    tile = tok_dev // shard_count
    targets = evening.reshape(shard_count)
    ids = jnp.arange(shard_count, dtype=jnp.int32)
    order = jnp.sum(jnp.where(targets[None, :] == ids[:, None], ids[None, :], 0), axis=1)
    mixed = jnp.concatenate(
        [lax.dynamic_slice_in_dim(mixed, order[d] * tile, tile, 0) for d in range(shard_count)]
    )
    mixed_full = lax.all_gather(mixed, "head", axis=1, tiled=True)
    outgoing = jnp.dot(mixed_full, full_proj, preferred_element_type=jnp.float32).astype(
        jnp.bfloat16
    )
    return lax.all_to_all(outgoing, "tok", split_axis=0, concat_axis=0, tiled=True)


def solution(mesh):
    return jax.shard_map(
        local,
        mesh=mesh,
        in_specs=(
            P("tok", "head"),
            P("tok", "head"),
            P("tok", "head"),
            P("tok", "head"),
            P("head", None, None),
            P("head", None, None),
            P("head", None, None),
            P("tok", "head"),
            P(),
            P("tok", None),
        ),
        out_specs=P("tok", "head"),
        check_vma=False,
    )
```

time: 616 us -> 566 us (0.919)
  matrix products: 91.2 us -> 35.1 us
  Pallas kernels: 0 us -> 21 us
  waiting for transfers between devices: 379 us -> 364 us
    reduce_scatter x0 -> x1, waiting for transfers between devices: none -> 117 us  [local(): total = lax.psum_scatter(grads, 'tok', scatter_dimension=0, tiled=True)]
    all_gather x1 -> x2, waiting for transfers between devices: 98 us -> 28.4 us  [the longest x1 28.4 us: local(): full_proj = lax.all_gather(out_proj, 'tok', axis=0, tiled=True)]
    ppermute x2 -> x4, waiting for transfers between devices: 206 us -> 160 us  [from_behind(): lax.ppermute(value, axis, [(source, source + steps) for source in range(l...]
    sub x2 -> x0, matrix products: 26.5 us -> none  [attend(): weights = jnp.exp(scores - top)]
    pallas_call x0 -> x1, Pallas kernels: none -> 21 us  [attention(): pl.pallas_call(attend_kernel, grid_spec=pltpu.PrefetchScalarGridSpec(num_...]
    dot_general x3 -> x1, matrix products: 34.7 us -> 13.7 us  [local(): jnp.dot(mixed_full, full_proj, preferred_element_type=jnp.float32)]
    psum x1 -> x0, waiting for transfers between devices: 15.9 us -> none  [local(): lax.psum((grad_one, grad_three, grad_two), 'tok')]
    unnamed x23 -> x34, local copies, waits for them, and re-layouts: 9.25 us -> 18.4 us
  transfers between devices with their start and end apart: 5 -> 8, of which waited for: 4 -> 5; matrix products, arithmetic and copies ran while one was open for 19% -> 9% of each run, Pallas kernels for 0% -> 4%
where the time goes in v1:
time: 566 us; the launch traced here: 565 us
  waiting for transfers between devices  364 us (64%)
  blocking collectives  53.9 us (10%)
  local copies, waits for them, and re-layouts  39.3 us (7%)
  matrix products  35.1 us (6%)
  Pallas kernels  21 us (4%)
  other arithmetic  19.4 us (3%)
  between operations  18.5 us (3%)
  starting transfers between devices  13.5 us (2%)
    ppermute x4, waiting for transfers between devices, from_behind(): lax.ppermute(value, axis, [(source, source + steps) for source in range(l...  160 us
    reduce_scatter x1, waiting for transfers between devices, local(): total = lax.psum_scatter(grads, 'tok', scatter_dimension=0, tiled=True)  117 us
    all_gather x1, waiting for transfers between devices, local(): mixed_full = lax.all_gather(mixed, 'head', axis=1, tiled=True)  57.9 us
    all_to_all x1, blocking collectives, local(): lax.all_to_all(outgoing, 'tok', split_axis=0, concat_axis=0, tiled=True)  53.9 us
    all_gather x1, waiting for transfers between devices, local(): full_proj = lax.all_gather(out_proj, 'tok', axis=0, tiled=True)  28.4 us
    pallas_call x1, Pallas kernels, attention(): pl.pallas_call(attend_kernel, grid_spec=pltpu.PrefetchScalarGridSpec(num_...  21 us
    unnamed x34, local copies, waits for them, and re-layouts  18.4 us
    dot_general x1, matrix products, local(): jnp.dot(mixed_full, full_proj, preferred_element_type=jnp.float32)  13.7 us
  transfers between devices with their start and end apart: 8, of which 5 were waited for; matrix products, arithmetic and copies ran while one was open for 9% of the time, Pallas kernels for 4%

profile of v1, /device:TPU:0, one launch (start us, length us, event | category | flops | bytes accessed | tf_op | source)
XLA Modules:
  0.0 565.2 jit_solution(10679143308961534382)
XLA Ops:
  6.5 2.9 copy.56
  9.9 3.0 copy.59
  12.9 2.6 multiply_convert_fusion.5
  22.9 2.4 fusion.4
  27.1 3.4 pad_maximum_fusion
  30.5 3.7 pad_maximum_fusion.1
  34.2 117.1 %reduce-scatter.2.cloned.1.call-done = f32[384,512]{1,0:T(8,128)} async-done(((f32[3072,512]{1,0:T(8,128)}), f32[384,512]{1,0:T(8,128)}) %reduce-scatter.2.cloned.1.call-update) | async-done | bytes 786448 | tf_op jit(solution)/shard_map/reduce_scatter | solution.py:127
  154.2 2.4 fusion.18
  156.6 4.8 collective-permute-start
  162.8 2.4 fusion.17
  165.1 5.8 %collective-permute-start.2 = (bf16[896,1024]{1,0:T(8,128)(2,1)}, bf16[896,1024]{1,0:T(8,128)(2,1)}, u32[]{:S(2)}, u32[]{:S(2)}) collective-permute-start(bf16[896,1024]{1,0:T(8,128)(2,1)} %get-tuple-element.11), channel_id=1, source_target_pairs={{0,1},{1,2},{2,3},{3,4},{4,5},{5,6},{6,7},{8,9},{9,10},{10,11},{11... | collective-permute-start | bytes 5505032 | tf_op jit(solution)/shard_map/ppermute | solution.py:16
  178.3 3.9 copy.64
  182.2 4.1 copy.67
  188.8 111.7 %collective-permute-done.kp_ref = bf16[896,1024]{1,0:T(8,128)(2,1)} collective-permute-done((bf16[896,1024]{1,0:T(8,128)(2,1)}, bf16[896,1024]{1,0:T(8,128)(2,1)}, u32[]{:S(2)}, u32[]{:S(2)}) %collective-permute-start) | collective-permute-done | bytes 1835040 | tf_op jit(solution)/shard_map/ppermute | solution.py:16
  300.5 48.7 %collective-permute-done.2.vp_ref = bf16[896,1024]{1,0:T(8,128)(2,1)} collective-permute-done((bf16[896,1024]{1,0:T(8,128)(2,1)}, bf16[896,1024]{1,0:T(8,128)(2,1)}, u32[]{:S(2)}, u32[]{:S(2)}) %collective-permute-start.2) | collective-permute-done | bytes 1835040 | tf_op jit(solution)/shard_map/ppermute | solution.py:16
  352.4 21.0 %shard_map.100 = f32[1024,1024]{1,0:T(8,128)} custom-call(s32[8]{0:T(128)S(1)} %get-tuple-element.23.first_ref, s32[8]{0:T(128)S(1)} %get-tuple-element.22.last_ref, bf16[1024,1024]{1,0:T(8,128)(2,1)S(1)} %copy-done.4, bf16[896,1024]{1,0:T(8,128)(2,1)} %collective-permute-done.kp_ref, bf16[1024,1024]{1,0:T(8,128)(2,1)S(1)} %copy-done, ...), custom_call_target="tpu_custom_call" | custom-call | flops 4294967296 | bytes 16777216 | tf_op jit(solution)/shard_map/pallas_call | solution.py:60
  376.6 3.2 fusion.8
  379.8 8.3 %fusion.7 = f32[2,512,1024]{2,1,0:T(8,128)} fusion(bf16[2,512,512]{2,1,0:T(8,128)(2,1)S(1)} %bitcast.67, f32[2,1024,512]{2,1,0:T(8,128)} %fusion.8, bf16[2,512,512]{2,1,0:T(8,128)(2,1)S(1)} %bitcast.66, f32[1024,2,512]{2,0,1:T(8,128)} %copy.67, f32[1024,2]{0,1:T(2,128)S(1)} %add_rsqrt_fusion), kind=kOutput, calls=%fused_computation.21 | convolution fusion | flops 2155872256 | bytes 14688256 | tf_op jit(solution)/shard_map/htf,hfd->thd/dot_general | solution.py:135
  388.1 5.3 copy.74
  393.5 4.3 add_convert_fusion
  403.5 28.4 %all-gather.8.cloned.1.call-done = bf16[4096,1024]{1,0:T(8,128)(2,1)} async-done(((bf16[512,1024]{1,0:T(8,128)(2,1)}), bf16[4096,1024]{1,0:T(8,128)(2,1)}) %all-gather.8.cloned.1.call-update) | async-done | bytes 8388624 | tf_op jit(solution)/shard_map/all_gather | solution.py:88
  431.9 57.9 %all-gather.6.cloned.1.call-done = bf16[1024,4096]{1,0:T(8,128)(2,1)} async-done(((bf16[1024,1024]{1,0:T(8,128)(2,1)}), bf16[1024,4096]{1,0:T(8,128)(2,1)}) %all-gather.6.cloned.1.call-update) | async-done | bytes 8388624 | tf_op jit(solution)/shard_map/all_gather | solution.py:147
  489.8 13.7 %convolution_convert_fusion = bf16[1024,1024]{1,0:T(8,128)(2,1)S(1)} fusion(bf16[1024,4096]{1,0:T(8,128)(2,1)} %all-gather.6.cloned.1.call-done, bf16[4096,1024]{1,0:T(8,128)(2,1)} %all-gather.8.cloned.1.call-done), kind=kOutput, calls=%fused_computation.17 | convolution fusion | flops 8590983168 | bytes 18874368 | tf_op jit(solution)/shard_map/dot_general | solution.py:148
  503.5 53.9 %all_to_all.12 = bf16[8,128,1024]{2,1,0:T(8,128)(2,1)S(1)} all-to-all(bf16[8,128,1024]{2,1,0:T(8,128)(2,1)S(1)} %bitcast.65), channel_id=1, replica_groups=mesh['head'=4,'tok'=8] {'tok'}, dimensions={0} | all-to-all | bytes 4194304 | tf_op jit(solution)/shard_map/all_to_all | solution.py:151
  (66 shorter events, 31.9 us)
Async XLA Ops:
  6.5 144.8 %reduce-scatter.2.cloned.1.call-start = ((), (), s32[]{:S(2)}) async-start(), calls=%async_computation.2 | async-start | bytes 7077888 | tf_op jit(solution)/shard_map/reduce_scatter | solution.py:127
  12.9 2.6 copy-start.7
  15.5 1.3 copy-start.6
  16.8 1.6 copy-start.1
  18.4 0.7 copy-start.9
  18.4 1.2 copy-start.8
  30.5 342.9 %all-gather.4.cloned.1.call-start = ((), (), s32[]{:S(2)}) async-start(), calls=%async_computation.3 | async-start | bytes 3538944 | tf_op jit(solution)/shard_map/all_gather | solution.py:130
  30.5 123.7 %copy-start = (bf16[1024,1024]{1,0:T(8,128)(2,1)S(1)}, bf16[1024,1024]{1,0:T(8,128)(2,1)}, u32[]{:S(2)}) copy-start(bf16[1024,1024]{1,0:T(8,128)(2,1)} %ko_ref.1) | copy-start | bytes 6291460
  153.4 278.5 %all-gather.8.cloned.1.call-start = ((), (), s32[]{:S(2)}) async-start(), calls=%async_computation.5 | async-start | bytes 9437184 | tf_op jit(solution)/shard_map/all_gather | solution.py:88
  154.2 335.6 %all-gather.6.cloned.1.call-start = ((), (), s32[]{:S(2)}) async-start(), calls=%async_computation.4 | async-start | bytes 10485760 | tf_op jit(solution)/shard_map/all_gather | solution.py:147
  154.2 8.5 %copy-start.2 = (bf16[1024,1024]{1,0:T(8,128)(2,1)S(1)}, bf16[1024,1024]{1,0:T(8,128)(2,1)}, u32[]{:S(2)}) copy-start(bf16[1024,1024]{1,0:T(8,128)(2,1)} %vo_ref.1) | copy-start | bytes 6291460
  156.6 15.8 %copy-start.10 = (s32[1,8]{1,0:T(1,128)S(1)}, s32[1,8]{1,0:T(1,128)}, u32[]{:S(2)}) copy-start(s32[1,8]{1,0:T(1,128)} %param.19) | copy-start | bytes 100
  156.6 143.9 %collective-permute-start = (bf16[896,1024]{1,0:T(8,128)(2,1)}, bf16[896,1024]{1,0:T(8,128)(2,1)}, u32[]{:S(2)}, u32[]{:S(2)}) collective-permute-start(bf16[896,1024]{1,0:T(8,128)(2,1)} %get-tuple-element.13), channel_id=1, source_target_pairs={{0,1},{1,2},{2,3},{3,4},{4,5},{5,6},{6,7},{8,9},{9,10},{10,11},{11... | collective-permute-start | bytes 5505032 | tf_op jit(solution)/shard_map/ppermute | solution.py:16
  161.5 139.0 %collective-permute-start.1 = (bf16[896,1024]{1,0:T(8,128)(2,1)}, bf16[896,1024]{1,0:T(8,128)(2,1)}, u32[]{:S(2)}, u32[]{:S(2)}) collective-permute-start(bf16[896,1024]{1,0:T(8,128)(2,1)} %get-tuple-element.12), channel_id=1, source_target_pairs={{1,0},{2,1},{3,2},{4,3},{5,4},{6,5},{7,6},{9,8},{10,9},{11,10},{12... | collective-permute-start | bytes 5505032 | tf_op jit(solution)/shard_map/ppermute | solution.py:16
  165.1 184.0 %collective-permute-start.2 = (bf16[896,1024]{1,0:T(8,128)(2,1)}, bf16[896,1024]{1,0:T(8,128)(2,1)}, u32[]{:S(2)}, u32[]{:S(2)}) collective-permute-start(bf16[896,1024]{1,0:T(8,128)(2,1)} %get-tuple-element.11), channel_id=1, source_target_pairs={{0,1},{1,2},{2,3},{3,4},{4,5},{5,6},{6,7},{8,9},{9,10},{10,11},{11... | collective-permute-start | bytes 5505032 | tf_op jit(solution)/shard_map/ppermute | solution.py:16
  170.9 178.3 %collective-permute-start.3 = (bf16[896,1024]{1,0:T(8,128)(2,1)}, bf16[896,1024]{1,0:T(8,128)(2,1)}, u32[]{:S(2)}, u32[]{:S(2)}) collective-permute-start(bf16[896,1024]{1,0:T(8,128)(2,1)} %get-tuple-element.10), channel_id=1, source_target_pairs={{1,0},{2,1},{3,2},{4,3},{5,4},{6,5},{7,6},{9,8},{10,9},{11,10},{12... | collective-permute-start | bytes 5505032 | tf_op jit(solution)/shard_map/ppermute | solution.py:16
  182.2 4.1 copy-start.11
  349.2 1.6 copy-start.3
  350.8 1.6 copy-start.4
  373.4 3.2 copy-start.5
Sparse Core Ops, SparseCore 0:
  30.6 120.6 reduce-scatter.1
  153.6 145.5 all-gather.3
  301.3 130.5 all-gather.7
  433.3 56.4 all-gather.5

commit v2 on v1

--- a/solution.py
+++ b/solution.py
@@ -14,6 +14,17 @@
     count = lax.axis_size(axis)
     leading, last = (max(0, -steps), min(count, count - steps))
     return lax.ppermute(value, axis, [(source, source + steps) for source in range(leading, last)])
+
+
+def around(value, axis, steps):
+    count = lax.axis_size(axis)
+    return lax.ppermute(value, axis, [(at, (at + steps) % count) for at in range(count)])
+
+
+def by_source(arrived, me):
+    count, rows = len(arrived), arrived[0].shape[0]
+    twice = jnp.concatenate(arrived[::-1] * 2)
+    return lax.dynamic_slice_in_dim(twice, (count - 1 - me) * rows, count * rows, 0)
 
 
 def rms_rows(rows):
@@ -124,10 +135,21 @@
     grads = jnp.stack([grad_one, grad_three, grad_two]).reshape(-1, DH)
     old = jnp.stack([fast_one, fast_three, fast_two]).reshape(-1, DH)
     share = grads.shape[0] // shard_count
-    total = lax.psum_scatter(grads, "tok", scatter_dimension=0, tiled=True)
+    block = lambda d: lax.dynamic_slice_in_dim(grads, (d % shard_count) * share, share, 0)
+    pieces = [
+        around(block(my_shard + r).astype(jnp.bfloat16), "tok", r) for r in range(1, shard_count)
+    ]
+    pieces, k_prev, k_next = lax.optimization_barrier((pieces, k_prev, k_next))
+    total = block(my_shard)
+    for piece in pieces:
+        total = total + piece.astype(jnp.float32)
     old_share = lax.dynamic_slice_in_dim(old, my_shard * share, share, 0)
     new_share = (old_share.astype(jnp.float32) - total).astype(jnp.bfloat16)
-    new = lax.all_gather(new_share, "tok", axis=0, tiled=True)
+    shares = [new_share] + [around(new_share, "tok", r) for r in range(1, shard_count)]
+    shares, v_prev, v_next, full_proj = lax.optimization_barrier(
+        (shares, v_prev, v_next, full_proj)
+    )
+    new = by_source(shares, my_shard)
     new_one, new_three, new_two = new.reshape((3,) + fast_one.shape)
     gate_q = jnp.einsum("thd,hdf->htf", query_norm, new_one, preferred_element_type=jnp.float32)
     up_q = jnp.einsum("thd,hdf->htf", query_norm, new_three, preferred_element_type=jnp.float32)
@@ -141,14 +163,21 @@
     targets = evening.reshape(shard_count)
     ids = jnp.arange(shard_count, dtype=jnp.int32)
     order = jnp.sum(jnp.where(targets[None, :] == ids[:, None], ids[None, :], 0), axis=1)
-    mixed = jnp.concatenate(
-        [lax.dynamic_slice_in_dim(mixed, order[d] * tile, tile, 0) for d in range(shard_count)]
-    )
-    mixed_full = lax.all_gather(mixed, "head", axis=1, tiled=True)
-    outgoing = jnp.dot(mixed_full, full_proj, preferred_element_type=jnp.float32).astype(
-        jnp.bfloat16
-    )
-    return lax.all_to_all(outgoing, "tok", split_axis=0, concat_axis=0, tiled=True)
+    steps = list(range(1, shard_count)) + [0]
+    half = shard_count // 2
+    arrived = {}
+    for group in (steps[:half], steps[half:]):
+        tiles = []
+        for r in group:
+            target = (my_shard + r) % shard_count
+            at = jnp.sum(jnp.where(ids == target, order, 0))
+            tiles.append(lax.dynamic_slice_in_dim(mixed, at * tile, tile, 0))
+        rows = lax.all_gather(jnp.concatenate(tiles), "head", axis=1, tiled=True)
+        out = jnp.dot(rows, full_proj, preferred_element_type=jnp.float32).astype(jnp.bfloat16)
+        for i, r in enumerate(group):
+            piece = out[i * tile : (i + 1) * tile]
+            arrived[r] = around(piece, "tok", r) if r else piece
+    return by_source([arrived[r] for r in range(shard_count)], my_shard)
 
 
 def solution(mesh):

time: 566 us -> 555 us (0.981)
  starting transfers between devices: 13.5 us -> 80.6 us
  blocking collectives: 53.9 us -> 0 us
  waiting for transfers between devices: 364 us -> 329 us
    ppermute x0 -> x21, waiting for transfers between devices: none -> 254 us  [around(): lax.ppermute(value, axis, [(at, (at + steps) % count) for at in range(cou...]
    ppermute x4, waiting for transfers between devices: 160 us -> 0.01 us  [from_behind(): lax.ppermute(value, axis, [(source, source + steps) for source in range(l...]
    reduce_scatter x1 -> x0, waiting for transfers between devices: 117 us -> none  [local(): total = lax.psum_scatter(grads, 'tok', scatter_dimension=0, tiled=True)]
    ppermute x0 -> x21, starting transfers between devices: none -> 59 us  [around(): lax.ppermute(value, axis, [(at, (at + steps) % count) for at in range(cou...]
    all_to_all x1 -> x0, blocking collectives: 53.9 us -> none  [local(): lax.all_to_all(outgoing, 'tok', split_axis=0, concat_axis=0, tiled=True)]
    all_gather x1, waiting for transfers between devices: 28.4 us -> 0.01 us  [local(): full_proj = lax.all_gather(out_proj, 'tok', axis=0, tiled=True)]
    all_gather x2, waiting for transfers between devices: 57.9 us -> 74.2 us  [local(): rows = lax.all_gather(jnp.concatenate(tiles), 'head', axis=1, tiled=True)]
    ppermute x4, starting transfers between devices: 13.3 us -> 21.3 us  [from_behind(): lax.ppermute(value, axis, [(source, source + steps) for source in range(l...]
  transfers between devices with their start and end apart: 8 -> 28, of which waited for: 5 -> 13; matrix products, arithmetic and copies ran while one was open for 9% -> 12% of each run, Pallas kernels for 4% -> 0%
where the time goes in v2:
time: 555 us; the launch traced here: 554 us
  waiting for transfers between devices  329 us (59%)
  starting transfers between devices  80.6 us (15%)
  local copies, waits for them, and re-layouts  43.9 us (8%)
  matrix products  40.1 us (7%)
  Pallas kernels  21.3 us (4%)
  other arithmetic  20.8 us (4%)
  between operations  18.6 us (3%)
    ppermute x21, waiting for transfers between devices, around(): lax.ppermute(value, axis, [(at, (at + steps) % count) for at in range(cou...  254 us
    all_gather x2, waiting for transfers between devices, local(): rows = lax.all_gather(jnp.concatenate(tiles), 'head', axis=1, tiled=True)  74.2 us
    ppermute x21, starting transfers between devices, around(): lax.ppermute(value, axis, [(at, (at + steps) % count) for at in range(cou...  59 us
    pallas_call x1, Pallas kernels, attention(): pl.pallas_call(attend_kernel, grid_spec=pltpu.PrefetchScalarGridSpec(num_...  21.3 us
    ppermute x4, starting transfers between devices, from_behind(): lax.ppermute(value, axis, [(source, source + steps) for source in range(l...  21.3 us
    unnamed x78, local copies, waits for them, and re-layouts  21.1 us
    dot_general x2, matrix products, local(): jnp.dot(rows, full_proj, preferred_element_type=jnp.float32)  18.3 us
  transfers between devices with their start and end apart: 28, of which 13 were waited for; matrix products, arithmetic and copies ran while one was open for 12% of the time, Pallas kernels for 0%

profile of v2, /device:TPU:0, one launch (start us, length us, event | category | flops | bytes accessed | tf_op | source)
XLA Modules:
  0.0 554.4 jit_solution(13975532270063821424)
XLA Ops:
  11.3 4.3 copy.59
  41.8 5.2 collective-permute-start.7
  52.2 8.5 %collective-permute-done = bf16[384,512]{1,0:T(8,128)(2,1)S(1)} collective-permute-done((bf16[384,512]{1,0:T(8,128)(2,1)S(1)}, bf16[384,512]{1,0:T(8,128)(2,1)S(1)}, u32[]{:S(2)}, u32[]{:S(2)}) %collective-permute-start) | collective-permute-done | bytes 393248 | tf_op jit(solution)/shard_map/ppermute | solution.py:21
  60.7 6.3 %collective-permute-start.3 = (bf16[384,512]{1,0:T(8,128)(2,1)S(1)}, bf16[384,512]{1,0:T(8,128)(2,1)}, u32[]{:S(2)}, u32[]{:S(2)}) collective-permute-start(bf16[384,512]{1,0:T(8,128)(2,1)S(1)} %get-tuple-element.61), channel_id=1, source_target_pairs={{0,4},{1,5},{2,6},{3,7},{4,0},{5,1},{6,2},{7,3},{8,12},{9,13},{10,... | collective-permute-start | bytes 1179656 | tf_op jit(solution)/shard_map/ppermute | solution.py:21
  67.0 68.9 %collective-permute-done.1 = bf16[384,512]{1,0:T(8,128)(2,1)} collective-permute-done((bf16[384,512]{1,0:T(8,128)(2,1)S(1)}, bf16[384,512]{1,0:T(8,128)(2,1)}, u32[]{:S(2)}, u32[]{:S(2)}) %collective-permute-start.1) | collective-permute-done | bytes 393248 | tf_op jit(solution)/shard_map/ppermute | solution.py:21
  135.9 18.4 %collective-permute-start.4 = (bf16[384,512]{1,0:T(8,128)(2,1)S(1)}, bf16[384,512]{1,0:T(8,128)(2,1)}, u32[]{:S(2)}, u32[]{:S(2)}) collective-permute-start(bf16[384,512]{1,0:T(8,128)(2,1)S(1)} %get-tuple-element.60), channel_id=1, source_target_pairs={{0,5},{1,6},{2,7},{3,0},{4,1},{5,2},{6,3},{7,4},{8,13},{9,14},{10,... | collective-permute-start | bytes 1179656 | tf_op jit(solution)/shard_map/ppermute | solution.py:21
  156.6 13.6 %collective-permute-start.16 = (bf16[896,1024]{1,0:T(8,128)(2,1)}, bf16[896,1024]{1,0:T(8,128)(2,1)}, u32[]{:S(2)}, u32[]{:S(2)}) collective-permute-start(bf16[896,1024]{1,0:T(8,128)(2,1)} %get-tuple-element.74), channel_id=1, source_target_pairs={{0,1},{1,2},{2,3},{3,4},{4,5},{5,6},{6,7},{8,9},{9,10},{10,11},{11... | collective-permute-start | bytes 5505032 | tf_op jit(solution)/shard_map/ppermute | solution.py:16
  170.2 21.7 %collective-permute-done.3 = bf16[384,512]{1,0:T(8,128)(2,1)} collective-permute-done((bf16[384,512]{1,0:T(8,128)(2,1)S(1)}, bf16[384,512]{1,0:T(8,128)(2,1)}, u32[]{:S(2)}, u32[]{:S(2)}) %collective-permute-start.3) | collective-permute-done | bytes 393248 | tf_op jit(solution)/shard_map/ppermute | solution.py:21
  196.2 79.2 %collective-permute-done.5 = bf16[384,512]{1,0:T(8,128)(2,1)} collective-permute-done((bf16[384,512]{1,0:T(8,128)(2,1)}, bf16[384,512]{1,0:T(8,128)(2,1)}, u32[]{:S(2)}, u32[]{:S(2)}) %collective-permute-start.5) | collective-permute-done | bytes 393248 | tf_op jit(solution)/shard_map/ppermute | solution.py:21
  278.2 8.5 %collective-permute-done.6 = bf16[384,512]{1,0:T(8,128)(2,1)S(1)} collective-permute-done((bf16[384,512]{1,0:T(8,128)(2,1)}, bf16[384,512]{1,0:T(8,128)(2,1)S(1)}, u32[]{:S(2)}, u32[]{:S(2)}) %collective-permute-start.6) | collective-permute-done | bytes 393248 | tf_op jit(solution)/shard_map/ppermute | solution.py:21
  304.2 8.4 %collective-permute-start.11 = (bf16[384,512]{1,0:T(8,128)(2,1)S(1)}, bf16[384,512]{1,0:T(8,128)(2,1)S(1)}, u32[]{:S(2)}, u32[]{:S(2)}) collective-permute-start(bf16[384,512]{1,0:T(8,128)(2,1)S(1)} %subtract_convert_fusion), channel_id=1, source_target_pairs={{0,3},{1,4},{2,5},{3,6},{4,7},{5,0},{6,1},{7,2},{8,11},{9,12},{10,... | collective-permute-start | bytes 1179656 | tf_op jit(solution)/shard_map/ppermute | solution.py:21
  318.0 18.9 %collective-permute-done.11 = bf16[384,512]{1,0:T(8,128)(2,1)S(1)} collective-permute-done((bf16[384,512]{1,0:T(8,128)(2,1)S(1)}, bf16[384,512]{1,0:T(8,128)(2,1)S(1)}, u32[]{:S(2)}, u32[]{:S(2)}) %collective-permute-start.11) | collective-permute-done | bytes 393248 | tf_op jit(solution)/shard_map/ppermute | solution.py:21
  337.0 7.7 %collective-permute-done.12 = bf16[384,512]{1,0:T(8,128)(2,1)S(1)} collective-permute-done((bf16[384,512]{1,0:T(8,128)(2,1)S(1)}, bf16[384,512]{1,0:T(8,128)(2,1)S(1)}, u32[]{:S(2)}, u32[]{:S(2)}) %collective-permute-start.12) | collective-permute-done | bytes 393248 | tf_op jit(solution)/shard_map/ppermute | solution.py:21
  348.3 5.4 collective-permute-done.15
  366.1 8.6 %fusion.7 = f32[2,512,1024]{2,1,0:T(8,128)} fusion(bf16[2,512,512]{2,1,0:T(8,128)(2,1)} %bitcast.58, f32[2,1024,512]{2,1,0:T(8,128)} %fusion.8, bf16[2,512,512]{2,1,0:T(8,128)(2,1)S(1)} %bitcast.57, f32[1024,2,512]{2,0,1:T(8,128)} %copy.67, f32[1024,2]{0,1:T(2,128)S(1)} %add_rsqrt_fusion), kind=kOutput, calls=%fused_computation.20 | convolution fusion | flops 2155872256 | bytes 14688256 | tf_op jit(solution)/shard_map/htf,hfd->thd/dot_general | solution.py:157
  374.7 5.4 copy.74
  383.2 21.3 %shard_map.100 = f32[1024,1024]{1,0:T(8,128)} custom-call(s32[8]{0:T(128)S(1)} %get-tuple-element.85.first_ref, s32[8]{0:T(128)S(1)} %get-tuple-element.84.last_ref, bf16[1024,1024]{1,0:T(8,128)(2,1)S(1)} %copy-done.4, bf16[896,1024]{1,0:T(8,128)(2,1)} %collective-permute-done.7.kp_ref, bf16[1024,1024]{1,0:T(8,128)(2,1)S(1)} %copy-done, ...), custom_call_target="tpu_custom_call" | custom-call | flops 4294967296 | bytes 16777216 | tf_op jit(solution)/shard_map/pallas_call | solution.py:71
  410.1 52.1 %all-gather.6.cloned.1.call-done = bf16[512,4096]{1,0:T(8,128)(2,1)} async-done(((bf16[512,1024]{1,0:T(8,128)(2,1)}), bf16[512,4096]{1,0:T(8,128)(2,1)}) %all-gather.6.cloned.1.call-update) | async-done | bytes 4194320 | tf_op jit(solution)/shard_map/all_gather | solution.py:175
  462.3 9.1 %convolution_convert_fusion.1 = bf16[512,1024]{1,0:T(8,128)(2,1)S(1)} fusion(bf16[512,4096]{1,0:T(8,128)(2,1)} %all-gather.6.cloned.1.call-done, bf16[4096,1024]{1,0:T(8,128)(2,1)} %all-gather.4.cloned.1.call-done), kind=kOutput, calls=%fused_computation.22 | convolution fusion | flops 4295491584 | bytes 13631488 | tf_op jit(solution)/shard_map/dot_general | solution.py:176
  471.5 4.3 collective-permute-start.18
  476.3 22.0 %all-gather.8.cloned.1.call-done = bf16[512,4096]{1,0:T(8,128)(2,1)} async-done(((bf16[512,1024]{1,0:T(8,128)(2,1)}), bf16[512,4096]{1,0:T(8,128)(2,1)}) %all-gather.8.cloned.1.call-update) | async-done | bytes 4194320 | tf_op jit(solution)/shard_map/all_gather | solution.py:175
  498.4 9.1 %convolution_convert_fusion = bf16[512,1024]{1,0:T(8,128)(2,1)S(1)} fusion(bf16[512,4096]{1,0:T(8,128)(2,1)} %all-gather.8.cloned.1.call-done, bf16[4096,1024]{1,0:T(8,128)(2,1)} %all-gather.4.cloned.1.call-done), kind=kOutput, calls=%fused_computation.21 | convolution fusion | flops 4295491584 | bytes 13631488 | tf_op jit(solution)/shard_map/dot_general | solution.py:176
  513.7 20.2 %collective-permute-done.21 = bf16[128,1024]{1,0:T(8,128)(2,1)S(1)} collective-permute-done((bf16[128,1024]{1,0:T(8,128)(2,1)S(1)}, bf16[128,1024]{1,0:T(8,128)(2,1)S(1)}, u32[]{:S(2)}, u32[]{:S(2)}) %collective-permute-start.21) | collective-permute-done | bytes 262176 | tf_op jit(solution)/shard_map/ppermute | solution.py:21
  533.9 12.1 %collective-permute-done.22 = bf16[128,1024]{1,0:T(8,128)(2,1)S(1)} collective-permute-done((bf16[128,1024]{1,0:T(8,128)(2,1)S(1)}, bf16[128,1024]{1,0:T(8,128)(2,1)S(1)}, u32[]{:S(2)}, u32[]{:S(2)}) %collective-permute-start.22) | collective-permute-done | bytes 262176 | tf_op jit(solution)/shard_map/ppermute | solution.py:21
  (157 shorter events, 96.3 us)
Async XLA Ops:
  6.5 347.1 %all-gather.4.cloned.1.call-start = ((), (), s32[]{:S(2)}) async-start(), calls=%async_computation | async-start | bytes 9437184 | tf_op jit(solution)/shard_map/all_gather | solution.py:99
  7.3 455.0 %all-gather.6.cloned.1.call-start = ((), (), s32[]{:S(2)}) async-start(), calls=%async_computation.1 | async-start | bytes 5242880 | tf_op jit(solution)/shard_map/all_gather | solution.py:175
  41.8 244.9 %collective-permute-start.7 = (bf16[896,1024]{1,0:T(8,128)(2,1)}, bf16[896,1024]{1,0:T(8,128)(2,1)}, u32[]{:S(2)}, u32[]{:S(2)}) collective-permute-start(bf16[896,1024]{1,0:T(8,128)(2,1)} %get-tuple-element.76), channel_id=1, source_target_pairs={{0,1},{1,2},{2,3},{3,4},{4,5},{5,6},{6,7},{8,9},{9,10},{10,11},{11... | collective-permute-start | bytes 5505032 | tf_op jit(solution)/shard_map/ppermute | solution.py:16
  46.9 239.8 %collective-permute-start.8 = (bf16[896,1024]{1,0:T(8,128)(2,1)}, bf16[896,1024]{1,0:T(8,128)(2,1)}, u32[]{:S(2)}, u32[]{:S(2)}) collective-permute-start(bf16[896,1024]{1,0:T(8,128)(2,1)} %get-tuple-element.75), channel_id=1, source_target_pairs={{1,0},{2,1},{3,2},{4,3},{5,4},{6,5},{7,6},{9,8},{10,9},{11,10},{12... | collective-permute-start | bytes 5505032 | tf_op jit(solution)/shard_map/ppermute | solution.py:16
  48.2 87.7 %collective-permute-start.1 = (bf16[384,512]{1,0:T(8,128)(2,1)S(1)}, bf16[384,512]{1,0:T(8,128)(2,1)}, u32[]{:S(2)}, u32[]{:S(2)}) collective-permute-start(bf16[384,512]{1,0:T(8,128)(2,1)S(1)} %get-tuple-element.63), channel_id=1, source_target_pairs={{0,2},{1,3},{2,4},{3,5},{4,6},{5,7},{6,0},{7,1},{8,10},{9,11},{10,... | collective-permute-start | bytes 1179656 | tf_op jit(solution)/shard_map/ppermute | solution.py:21
  50.7 106.0 %collective-permute-start.2 = (bf16[384,512]{1,0:T(8,128)(2,1)S(1)}, bf16[384,512]{1,0:T(8,128)(2,1)}, u32[]{:S(2)}, u32[]{:S(2)}) collective-permute-start(bf16[384,512]{1,0:T(8,128)(2,1)S(1)} %get-tuple-element.62), channel_id=1, source_target_pairs={{0,3},{1,4},{2,5},{3,6},{4,7},{5,0},{6,1},{7,2},{8,11},{9,12},{10,... | collective-permute-start | bytes 1179656 | tf_op jit(solution)/shard_map/ppermute | solution.py:21
  60.7 131.3 %collective-permute-start.3 = (bf16[384,512]{1,0:T(8,128)(2,1)S(1)}, bf16[384,512]{1,0:T(8,128)(2,1)}, u32[]{:S(2)}, u32[]{:S(2)}) collective-permute-start(bf16[384,512]{1,0:T(8,128)(2,1)S(1)} %get-tuple-element.61), channel_id=1, source_target_pairs={{0,4},{1,5},{2,6},{3,7},{4,0},{5,1},{6,2},{7,3},{8,12},{9,13},{10,... | collective-permute-start | bytes 1179656 | tf_op jit(solution)/shard_map/ppermute | solution.py:21
  135.9 57.3 %collective-permute-start.4 = (bf16[384,512]{1,0:T(8,128)(2,1)S(1)}, bf16[384,512]{1,0:T(8,128)(2,1)}, u32[]{:S(2)}, u32[]{:S(2)}) collective-permute-start(bf16[384,512]{1,0:T(8,128)(2,1)S(1)} %get-tuple-element.60), channel_id=1, source_target_pairs={{0,5},{1,6},{2,7},{3,0},{4,1},{5,2},{6,3},{7,4},{8,13},{9,14},{10,... | collective-permute-start | bytes 1179656 | tf_op jit(solution)/shard_map/ppermute | solution.py:21
  156.6 156.0 %collective-permute-start.16 = (bf16[896,1024]{1,0:T(8,128)(2,1)}, bf16[896,1024]{1,0:T(8,128)(2,1)}, u32[]{:S(2)}, u32[]{:S(2)}) collective-permute-start(bf16[896,1024]{1,0:T(8,128)(2,1)} %get-tuple-element.74), channel_id=1, source_target_pairs={{0,1},{1,2},{2,3},{3,4},{4,5},{5,6},{6,7},{8,9},{9,10},{10,11},{11... | collective-permute-start | bytes 5505032 | tf_op jit(solution)/shard_map/ppermute | solution.py:16
  192.0 120.7 %collective-permute-start.17 = (bf16[896,1024]{1,0:T(8,128)(2,1)}, bf16[896,1024]{1,0:T(8,128)(2,1)}, u32[]{:S(2)}, u32[]{:S(2)}) collective-permute-start(bf16[896,1024]{1,0:T(8,128)(2,1)} %get-tuple-element.73), channel_id=1, source_target_pairs={{1,0},{2,1},{3,2},{4,3},{5,4},{6,5},{7,6},{9,8},{10,9},{11,10},{12... | collective-permute-start | bytes 5505032 | tf_op jit(solution)/shard_map/ppermute | solution.py:16
  193.3 82.1 %collective-permute-start.5 = (bf16[384,512]{1,0:T(8,128)(2,1)}, bf16[384,512]{1,0:T(8,128)(2,1)}, u32[]{:S(2)}, u32[]{:S(2)}) collective-permute-start(bf16[384,512]{1,0:T(8,128)(2,1)} %get-tuple-element.59), channel_id=1, source_target_pairs={{0,6},{1,7},{2,0},{3,1},{4,2},{5,3},{6,4},{7,5},{8,14},{9,15},{10,... | collective-permute-start | bytes 1179656 | tf_op jit(solution)/shard_map/ppermute | solution.py:21
  304.2 32.7 %collective-permute-start.11 = (bf16[384,512]{1,0:T(8,128)(2,1)S(1)}, bf16[384,512]{1,0:T(8,128)(2,1)S(1)}, u32[]{:S(2)}, u32[]{:S(2)}) collective-permute-start(bf16[384,512]{1,0:T(8,128)(2,1)S(1)} %subtract_convert_fusion), channel_id=1, source_target_pairs={{0,3},{1,4},{2,5},{3,6},{4,7},{5,0},{6,1},{7,2},{8,11},{9,12},{10,... | collective-permute-start | bytes 1179656 | tf_op jit(solution)/shard_map/ppermute | solution.py:21
  312.6 32.1 %collective-permute-start.12 = (bf16[384,512]{1,0:T(8,128)(2,1)S(1)}, bf16[384,512]{1,0:T(8,128)(2,1)S(1)}, u32[]{:S(2)}, u32[]{:S(2)}) collective-permute-start(bf16[384,512]{1,0:T(8,128)(2,1)S(1)} %subtract_convert_fusion), channel_id=1, source_target_pairs={{0,4},{1,5},{2,6},{3,7},{4,0},{5,1},{6,2},{7,3},{8,12},{9,13},{10,... | collective-permute-start | bytes 1179656 | tf_op jit(solution)/shard_map/ppermute | solution.py:21
  312.6 32.1 %collective-permute-start.13 = (bf16[384,512]{1,0:T(8,128)(2,1)S(1)}, bf16[384,512]{1,0:T(8,128)(2,1)S(1)}, u32[]{:S(2)}, u32[]{:S(2)}) collective-permute-start(bf16[384,512]{1,0:T(8,128)(2,1)S(1)} %subtract_convert_fusion), channel_id=1, source_target_pairs={{0,5},{1,6},{2,7},{3,0},{4,1},{5,2},{6,3},{7,4},{8,13},{9,14},{10,... | collective-permute-start | bytes 1179656 | tf_op jit(solution)/shard_map/ppermute | solution.py:21
  315.1 32.5 %collective-permute-start.14 = (bf16[384,512]{1,0:T(8,128)(2,1)S(1)}, bf16[384,512]{1,0:T(8,128)(2,1)S(1)}, u32[]{:S(2)}, u32[]{:S(2)}) collective-permute-start(bf16[384,512]{1,0:T(8,128)(2,1)S(1)} %subtract_convert_fusion), channel_id=1, source_target_pairs={{0,6},{1,7},{2,0},{3,1},{4,2},{5,3},{6,4},{7,5},{8,14},{9,15},{10,... | collective-permute-start | bytes 1179656 | tf_op jit(solution)/shard_map/ppermute | solution.py:21
  315.2 38.5 %collective-permute-start.15 = (bf16[384,512]{1,0:T(8,128)(2,1)S(1)}, bf16[384,512]{1,0:T(8,128)(2,1)}, u32[]{:S(2)}, u32[]{:S(2)}) collective-permute-start(bf16[384,512]{1,0:T(8,128)(2,1)S(1)} %subtract_convert_fusion), channel_id=1, source_target_pairs={{0,7},{1,0},{2,1},{3,2},{4,3},{5,4},{6,5},{7,6},{8,15},{9,8},{10,9... | collective-permute-start | bytes 1179656 | tf_op jit(solution)/shard_map/ppermute | solution.py:21
  408.8 89.6 %all-gather.8.cloned.1.call-start = ((), (), s32[]{:S(2)}) async-start(), calls=%async_computation.2 | async-start | bytes 5242880 | tf_op jit(solution)/shard_map/all_gather | solution.py:175
  471.5 41.0 %collective-permute-start.18 = (bf16[128,1024]{1,0:T(8,128)(2,1)S(1)}, bf16[128,1024]{1,0:T(8,128)(2,1)S(1)}, u32[]{:S(2)}, u32[]{:S(2)}) collective-permute-start(bf16[128,1024]{1,0:T(8,128)(2,1)S(1)} %get-tuple-element.83), channel_id=1, source_target_pairs={{0,7},{1,0},{2,1},{3,2},{4,3},{5,4},{6,5},{7,6},{8,15},{9,8},{10,9... | collective-permute-start | bytes 786440 | tf_op jit(solution)/shard_map/ppermute | solution.py:21
  475.8 36.7 %collective-permute-start.19 = (bf16[128,1024]{1,0:T(8,128)(2,1)S(1)}, bf16[128,1024]{1,0:T(8,128)(2,1)S(1)}, u32[]{:S(2)}, u32[]{:S(2)}) collective-permute-start(bf16[128,1024]{1,0:T(8,128)(2,1)S(1)} %get-tuple-element.82), channel_id=1, source_target_pairs={{0,6},{1,7},{2,0},{3,1},{4,2},{5,3},{6,4},{7,5},{8,14},{9,15},{10,... | collective-permute-start | bytes 786440 | tf_op jit(solution)/shard_map/ppermute | solution.py:21
  476.3 37.3 %collective-permute-start.20 = (bf16[128,1024]{1,0:T(8,128)(2,1)S(1)}, bf16[128,1024]{1,0:T(8,128)(2,1)S(1)}, u32[]{:S(2)}, u32[]{:S(2)}) collective-permute-start(bf16[128,1024]{1,0:T(8,128)(2,1)S(1)} %get-tuple-element.81), channel_id=1, source_target_pairs={{0,5},{1,6},{2,7},{3,0},{4,1},{5,2},{6,3},{7,4},{8,13},{9,14},{10,... | collective-permute-start | bytes 786440 | tf_op jit(solution)/shard_map/ppermute | solution.py:21
  507.6 26.3 %collective-permute-start.21 = (bf16[128,1024]{1,0:T(8,128)(2,1)S(1)}, bf16[128,1024]{1,0:T(8,128)(2,1)S(1)}, u32[]{:S(2)}, u32[]{:S(2)}) collective-permute-start(bf16[128,1024]{1,0:T(8,128)(2,1)S(1)} %get-tuple-element.80), channel_id=1, source_target_pairs={{0,4},{1,5},{2,6},{3,7},{4,0},{5,1},{6,2},{7,3},{8,12},{9,13},{10,... | collective-permute-start | bytes 786440 | tf_op jit(solution)/shard_map/ppermute | solution.py:21
  510.1 35.9 %collective-permute-start.22 = (bf16[128,1024]{1,0:T(8,128)(2,1)S(1)}, bf16[128,1024]{1,0:T(8,128)(2,1)S(1)}, u32[]{:S(2)}, u32[]{:S(2)}) collective-permute-start(bf16[128,1024]{1,0:T(8,128)(2,1)S(1)} %get-tuple-element.79), channel_id=1, source_target_pairs={{0,3},{1,4},{2,5},{3,6},{4,7},{5,0},{6,1},{7,2},{8,11},{9,12},{10,... | collective-permute-start | bytes 786440 | tf_op jit(solution)/shard_map/ppermute | solution.py:21
  512.5 33.6 %collective-permute-start.23 = (bf16[128,1024]{1,0:T(8,128)(2,1)S(1)}, bf16[128,1024]{1,0:T(8,128)(2,1)S(1)}, u32[]{:S(2)}, u32[]{:S(2)}) collective-permute-start(bf16[128,1024]{1,0:T(8,128)(2,1)S(1)} %get-tuple-element.78), channel_id=1, source_target_pairs={{0,2},{1,3},{2,4},{3,5},{4,6},{5,7},{6,0},{7,1},{8,10},{9,11},{10,... | collective-permute-start | bytes 786440 | tf_op jit(solution)/shard_map/ppermute | solution.py:21
  512.5 33.6 %collective-permute-start.24 = (bf16[128,1024]{1,0:T(8,128)(2,1)S(1)}, bf16[128,1024]{1,0:T(8,128)(2,1)S(1)}, u32[]{:S(2)}, u32[]{:S(2)}) collective-permute-start(bf16[128,1024]{1,0:T(8,128)(2,1)S(1)} %get-tuple-element.77), channel_id=1, source_target_pairs={{0,1},{1,2},{2,3},{3,4},{4,5},{5,6},{6,7},{7,0},{8,9},{9,10},{10,1... | collective-permute-start | bytes 786440 | tf_op jit(solution)/shard_map/ppermute | solution.py:21
  (27 other events, 690.9 us)
Sparse Core Ops, SparseCore 0:
  9.5 232.5 all-gather.3
  408.9 53.3 all-gather.5
  463.8 34.4 all-gather.7

commit v3 on v2

--- a/solution.py
+++ b/solution.py
@@ -165,16 +165,17 @@
     order = jnp.sum(jnp.where(targets[None, :] == ids[:, None], ids[None, :], 0), axis=1)
     steps = list(range(1, shard_count)) + [0]
     half = shard_count // 2
+    tiles = []
+    for r in steps:
+        target = (my_shard + r) % shard_count
+        at = jnp.sum(jnp.where(ids == target, order, 0))
+        tiles.append(lax.dynamic_slice_in_dim(mixed, at * tile, tile, 0))
+    rows = lax.all_gather(jnp.concatenate(tiles), "head", axis=1, tiled=True)
     arrived = {}
-    for group in (steps[:half], steps[half:]):
-        tiles = []
-        for r in group:
-            target = (my_shard + r) % shard_count
-            at = jnp.sum(jnp.where(ids == target, order, 0))
-            tiles.append(lax.dynamic_slice_in_dim(mixed, at * tile, tile, 0))
-        rows = lax.all_gather(jnp.concatenate(tiles), "head", axis=1, tiled=True)
-        out = jnp.dot(rows, full_proj, preferred_element_type=jnp.float32).astype(jnp.bfloat16)
-        for i, r in enumerate(group):
+    for begin in (0, half):
+        part = rows[begin * tile : (begin + half) * tile]
+        out = jnp.dot(part, full_proj, preferred_element_type=jnp.float32).astype(jnp.bfloat16)
+        for i, r in enumerate(steps[begin : begin + half]):
             piece = out[i * tile : (i + 1) * tile]
             arrived[r] = around(piece, "tok", r) if r else piece
     return by_source([arrived[r] for r in range(shard_count)], my_shard)

time: 555 us -> 556 us (level)
    all_gather x2 -> x1, waiting for transfers between devices: 74.2 us -> 77.3 us  [local(): rows = lax.all_gather(jnp.concatenate(tiles), 'head', axis=1, tiled=True)]
    unnamed x78 -> x89, local copies, waits for them, and re-layouts: 21.1 us -> 22.6 us
  transfers between devices with their start and end apart: 28 -> 27, of which waited for: 13 -> 13; matrix products, arithmetic and copies ran while one was open for 12% -> 10% of each run, Pallas kernels for 0% -> 0%
where the time goes in v3:
time: 556 us; the launch traced here: 555 us
  waiting for transfers between devices  332 us (60%)
  starting transfers between devices  80.4 us (14%)
  local copies, waits for them, and re-layouts  45.3 us (8%)
  matrix products  38.1 us (7%)
  Pallas kernels  21.3 us (4%)
  between operations  19 us (3%)
  other arithmetic  18.7 us (3%)
    ppermute x21, waiting for transfers between devices, around(): lax.ppermute(value, axis, [(at, (at + steps) % count) for at in range(cou...  254 us
    all_gather x1, waiting for transfers between devices, local(): rows = lax.all_gather(jnp.concatenate(tiles), 'head', axis=1, tiled=True)  77.3 us
    ppermute x21, starting transfers between devices, around(): lax.ppermute(value, axis, [(at, (at + steps) % count) for at in range(cou...  59 us
    unnamed x89, local copies, waits for them, and re-layouts  22.6 us
    ppermute x4, starting transfers between devices, from_behind(): lax.ppermute(value, axis, [(source, source + steps) for source in range(l...  21.3 us
    pallas_call x1, Pallas kernels, attention(): pl.pallas_call(attend_kernel, grid_spec=pltpu.PrefetchScalarGridSpec(num_...  21.3 us
    dot_general x2, matrix products, local(): jnp.dot(part, full_proj, preferred_element_type=jnp.float32)  16.4 us
  transfers between devices with their start and end apart: 27, of which 13 were waited for; matrix products, arithmetic and copies ran while one was open for 10% of the time, Pallas kernels for 0%

profile of v3, /device:TPU:0, one launch (start us, length us, event | category | flops | bytes accessed | tf_op | source)
XLA Modules:
  0.0 554.6 jit_solution(7473886341284937112)
XLA Ops:
  11.3 4.3 copy.59
  41.8 5.2 collective-permute-start.7
  52.2 8.5 %collective-permute-done = bf16[384,512]{1,0:T(8,128)(2,1)S(1)} collective-permute-done((bf16[384,512]{1,0:T(8,128)(2,1)S(1)}, bf16[384,512]{1,0:T(8,128)(2,1)S(1)}, u32[]{:S(2)}, u32[]{:S(2)}) %collective-permute-start) | collective-permute-done | bytes 393248 | tf_op jit(solution)/shard_map/ppermute | solution.py:21
  60.7 6.3 %collective-permute-start.3 = (bf16[384,512]{1,0:T(8,128)(2,1)S(1)}, bf16[384,512]{1,0:T(8,128)(2,1)}, u32[]{:S(2)}, u32[]{:S(2)}) collective-permute-start(bf16[384,512]{1,0:T(8,128)(2,1)S(1)} %get-tuple-element.61), channel_id=1, source_target_pairs={{0,4},{1,5},{2,6},{3,7},{4,0},{5,1},{6,2},{7,3},{8,12},{9,13},{10,... | collective-permute-start | bytes 1179656 | tf_op jit(solution)/shard_map/ppermute | solution.py:21
  67.0 68.9 %collective-permute-done.1 = bf16[384,512]{1,0:T(8,128)(2,1)} collective-permute-done((bf16[384,512]{1,0:T(8,128)(2,1)S(1)}, bf16[384,512]{1,0:T(8,128)(2,1)}, u32[]{:S(2)}, u32[]{:S(2)}) %collective-permute-start.1) | collective-permute-done | bytes 393248 | tf_op jit(solution)/shard_map/ppermute | solution.py:21
  135.9 18.4 %collective-permute-start.4 = (bf16[384,512]{1,0:T(8,128)(2,1)S(1)}, bf16[384,512]{1,0:T(8,128)(2,1)}, u32[]{:S(2)}, u32[]{:S(2)}) collective-permute-start(bf16[384,512]{1,0:T(8,128)(2,1)S(1)} %get-tuple-element.60), channel_id=1, source_target_pairs={{0,5},{1,6},{2,7},{3,0},{4,1},{5,2},{6,3},{7,4},{8,13},{9,14},{10,... | collective-permute-start | bytes 1179656 | tf_op jit(solution)/shard_map/ppermute | solution.py:21
  156.6 13.6 %collective-permute-start.16 = (bf16[896,1024]{1,0:T(8,128)(2,1)}, bf16[896,1024]{1,0:T(8,128)(2,1)}, u32[]{:S(2)}, u32[]{:S(2)}) collective-permute-start(bf16[896,1024]{1,0:T(8,128)(2,1)} %get-tuple-element.66), channel_id=1, source_target_pairs={{0,1},{1,2},{2,3},{3,4},{4,5},{5,6},{6,7},{8,9},{9,10},{10,11},{11... | collective-permute-start | bytes 5505032 | tf_op jit(solution)/shard_map/ppermute | solution.py:16
  170.2 21.7 %collective-permute-done.3 = bf16[384,512]{1,0:T(8,128)(2,1)} collective-permute-done((bf16[384,512]{1,0:T(8,128)(2,1)S(1)}, bf16[384,512]{1,0:T(8,128)(2,1)}, u32[]{:S(2)}, u32[]{:S(2)}) %collective-permute-start.3) | collective-permute-done | bytes 393248 | tf_op jit(solution)/shard_map/ppermute | solution.py:21
  196.2 79.2 %collective-permute-done.5 = bf16[384,512]{1,0:T(8,128)(2,1)} collective-permute-done((bf16[384,512]{1,0:T(8,128)(2,1)}, bf16[384,512]{1,0:T(8,128)(2,1)}, u32[]{:S(2)}, u32[]{:S(2)}) %collective-permute-start.5) | collective-permute-done | bytes 393248 | tf_op jit(solution)/shard_map/ppermute | solution.py:21
  278.2 8.5 %collective-permute-done.6 = bf16[384,512]{1,0:T(8,128)(2,1)S(1)} collective-permute-done((bf16[384,512]{1,0:T(8,128)(2,1)}, bf16[384,512]{1,0:T(8,128)(2,1)S(1)}, u32[]{:S(2)}, u32[]{:S(2)}) %collective-permute-start.6) | collective-permute-done | bytes 393248 | tf_op jit(solution)/shard_map/ppermute | solution.py:21
  297.9 4.1 copy.67
  304.3 8.4 %collective-permute-start.11 = (bf16[384,512]{1,0:T(8,128)(2,1)S(1)}, bf16[384,512]{1,0:T(8,128)(2,1)S(1)}, u32[]{:S(2)}, u32[]{:S(2)}) collective-permute-start(bf16[384,512]{1,0:T(8,128)(2,1)S(1)} %subtract_convert_fusion), channel_id=1, source_target_pairs={{0,3},{1,4},{2,5},{3,6},{4,7},{5,0},{6,1},{7,2},{8,11},{9,12},{10,... | collective-permute-start | bytes 1179656 | tf_op jit(solution)/shard_map/ppermute | solution.py:21
  318.1 18.9 %collective-permute-done.11 = bf16[384,512]{1,0:T(8,128)(2,1)S(1)} collective-permute-done((bf16[384,512]{1,0:T(8,128)(2,1)S(1)}, bf16[384,512]{1,0:T(8,128)(2,1)S(1)}, u32[]{:S(2)}, u32[]{:S(2)}) %collective-permute-start.11) | collective-permute-done | bytes 393248 | tf_op jit(solution)/shard_map/ppermute | solution.py:21
  336.9 7.8 %collective-permute-done.12 = bf16[384,512]{1,0:T(8,128)(2,1)S(1)} collective-permute-done((bf16[384,512]{1,0:T(8,128)(2,1)S(1)}, bf16[384,512]{1,0:T(8,128)(2,1)S(1)}, u32[]{:S(2)}, u32[]{:S(2)}) %collective-permute-start.12) | collective-permute-done | bytes 393248 | tf_op jit(solution)/shard_map/ppermute | solution.py:21
  348.3 5.4 collective-permute-done.15
  366.1 8.6 %fusion.11 = f32[2,512,1024]{2,1,0:T(8,128)} fusion(bf16[2,512,512]{2,1,0:T(8,128)(2,1)} %bitcast.56, f32[2,1024,512]{2,1,0:T(8,128)} %fusion.18, bf16[2,512,512]{2,1,0:T(8,128)(2,1)S(1)} %bitcast.55, f32[1024,2,512]{2,0,1:T(8,128)} %copy.67, f32[1024,2]{0,1:T(2,128)S(1)} %add_rsqrt_fusion), kind=kOutput, calls=%fused_computation.24 | convolution fusion | flops 2155872256 | bytes 14688256 | tf_op jit(solution)/shard_map/htf,hfd->thd/dot_general | solution.py:157
  374.7 5.4 copy.74
  383.3 21.3 %shard_map.100 = f32[1024,1024]{1,0:T(8,128)} custom-call(s32[8]{0:T(128)S(1)} %get-tuple-element.77.first_ref, s32[8]{0:T(128)S(1)} %get-tuple-element.76.last_ref, bf16[1024,1024]{1,0:T(8,128)(2,1)S(1)} %copy-done.4, bf16[896,1024]{1,0:T(8,128)(2,1)} %collective-permute-done.7.kp_ref, bf16[1024,1024]{1,0:T(8,128)(2,1)S(1)} %copy-done, ...), custom_call_target="tpu_custom_call" | custom-call | flops 4294967296 | bytes 16777216 | tf_op jit(solution)/shard_map/pallas_call | solution.py:71
  409.2 77.3 %all-gather.5.cloned.1.call-done = bf16[1024,4096]{1,0:T(8,128)(2,1)} async-done(((bf16[1024,1024]{1,0:T(8,128)(2,1)}), bf16[1024,4096]{1,0:T(8,128)(2,1)}) %all-gather.5.cloned.1.call-update) | async-done | bytes 8388624 | tf_op jit(solution)/shard_map/all_gather | solution.py:173
  486.5 9.3 %fusion.12 = bf16[512,1024]{1,0:T(8,128)(2,1)S(1)} fusion(bf16[4096,1024]{1,0:T(8,128)(2,1)} %all-gather.3.cloned.1.call-done, bf16[1024,4096]{1,0:T(8,128)(2,1)} %all-gather.5.cloned.1.call-done), kind=kOutput, calls=%fused_computation.25 | convolution fusion | flops 4295491584 | bytes 13631488 | tf_op jit(solution)/shard_map/dot_general | solution.py:177
  495.8 4.3 collective-permute-start.18
  500.6 7.1 %fusion.15 = bf16[512,1024]{1,0:T(8,128)(2,1)S(1)} fusion(bf16[4096,1024]{1,0:T(8,128)(2,1)} %all-gather.3.cloned.1.call-done, bf16[1024,4096]{1,0:T(8,128)(2,1)S(1)} %copy-done.22), kind=kOutput, calls=%fused_computation.26 | convolution fusion | flops 4295491584 | bytes 13631488 | tf_op jit(solution)/shard_map/dot_general | solution.py:177
  513.9 4.2 collective-permute-done.20
  518.1 27.4 %collective-permute-done.21 = bf16[128,1024]{1,0:T(8,128)(2,1)S(1)} collective-permute-done((bf16[128,1024]{1,0:T(8,128)(2,1)S(1)}, bf16[128,1024]{1,0:T(8,128)(2,1)S(1)}, u32[]{:S(2)}, u32[]{:S(2)}) %collective-permute-start.21) | collective-permute-done | bytes 262176 | tf_op jit(solution)/shard_map/ppermute | solution.py:21
  (163 shorter events, 91.6 us)
Async XLA Ops:
  6.5 347.2 %all-gather.3.cloned.1.call-start = ((), (), s32[]{:S(2)}) async-start(), calls=%async_computation | async-start | bytes 9437184 | tf_op jit(solution)/shard_map/all_gather | solution.py:99
  7.3 479.2 %all-gather.5.cloned.1.call-start = ((), (), s32[]{:S(2)}) async-start(), calls=%async_computation.1 | async-start | bytes 10485760 | tf_op jit(solution)/shard_map/all_gather | solution.py:173
  36.6 24.2 %collective-permute-start = (bf16[384,512]{1,0:T(8,128)(2,1)S(1)}, bf16[384,512]{1,0:T(8,128)(2,1)S(1)}, u32[]{:S(2)}, u32[]{:S(2)}) collective-permute-start(bf16[384,512]{1,0:T(8,128)(2,1)S(1)} %get-tuple-element.64), channel_id=1, source_target_pairs={{0,1},{1,2},{2,3},{3,4},{4,5},{5,6},{6,7},{7,0},{8,9},{9,10},{10,1... | collective-permute-start | bytes 1179656 | tf_op jit(solution)/shard_map/ppermute | solution.py:21
  41.8 244.9 %collective-permute-start.7 = (bf16[896,1024]{1,0:T(8,128)(2,1)}, bf16[896,1024]{1,0:T(8,128)(2,1)}, u32[]{:S(2)}, u32[]{:S(2)}) collective-permute-start(bf16[896,1024]{1,0:T(8,128)(2,1)} %get-tuple-element.68), channel_id=1, source_target_pairs={{0,1},{1,2},{2,3},{3,4},{4,5},{5,6},{6,7},{8,9},{9,10},{10,11},{11... | collective-permute-start | bytes 5505032 | tf_op jit(solution)/shard_map/ppermute | solution.py:16
  46.9 239.8 %collective-permute-start.8 = (bf16[896,1024]{1,0:T(8,128)(2,1)}, bf16[896,1024]{1,0:T(8,128)(2,1)}, u32[]{:S(2)}, u32[]{:S(2)}) collective-permute-start(bf16[896,1024]{1,0:T(8,128)(2,1)} %get-tuple-element.67), channel_id=1, source_target_pairs={{1,0},{2,1},{3,2},{4,3},{5,4},{6,5},{7,6},{9,8},{10,9},{11,10},{12... | collective-permute-start | bytes 5505032 | tf_op jit(solution)/shard_map/ppermute | solution.py:16
  48.2 87.7 %collective-permute-start.1 = (bf16[384,512]{1,0:T(8,128)(2,1)S(1)}, bf16[384,512]{1,0:T(8,128)(2,1)}, u32[]{:S(2)}, u32[]{:S(2)}) collective-permute-start(bf16[384,512]{1,0:T(8,128)(2,1)S(1)} %get-tuple-element.63), channel_id=1, source_target_pairs={{0,2},{1,3},{2,4},{3,5},{4,6},{5,7},{6,0},{7,1},{8,10},{9,11},{10,... | collective-permute-start | bytes 1179656 | tf_op jit(solution)/shard_map/ppermute | solution.py:21
  50.7 106.0 %collective-permute-start.2 = (bf16[384,512]{1,0:T(8,128)(2,1)S(1)}, bf16[384,512]{1,0:T(8,128)(2,1)}, u32[]{:S(2)}, u32[]{:S(2)}) collective-permute-start(bf16[384,512]{1,0:T(8,128)(2,1)S(1)} %get-tuple-element.62), channel_id=1, source_target_pairs={{0,3},{1,4},{2,5},{3,6},{4,7},{5,0},{6,1},{7,2},{8,11},{9,12},{10,... | collective-permute-start | bytes 1179656 | tf_op jit(solution)/shard_map/ppermute | solution.py:21
  60.7 131.2 %collective-permute-start.3 = (bf16[384,512]{1,0:T(8,128)(2,1)S(1)}, bf16[384,512]{1,0:T(8,128)(2,1)}, u32[]{:S(2)}, u32[]{:S(2)}) collective-permute-start(bf16[384,512]{1,0:T(8,128)(2,1)S(1)} %get-tuple-element.61), channel_id=1, source_target_pairs={{0,4},{1,5},{2,6},{3,7},{4,0},{5,1},{6,2},{7,3},{8,12},{9,13},{10,... | collective-permute-start | bytes 1179656 | tf_op jit(solution)/shard_map/ppermute | solution.py:21
  135.9 57.3 %collective-permute-start.4 = (bf16[384,512]{1,0:T(8,128)(2,1)S(1)}, bf16[384,512]{1,0:T(8,128)(2,1)}, u32[]{:S(2)}, u32[]{:S(2)}) collective-permute-start(bf16[384,512]{1,0:T(8,128)(2,1)S(1)} %get-tuple-element.60), channel_id=1, source_target_pairs={{0,5},{1,6},{2,7},{3,0},{4,1},{5,2},{6,3},{7,4},{8,13},{9,14},{10,... | collective-permute-start | bytes 1179656 | tf_op jit(solution)/shard_map/ppermute | solution.py:21
  156.6 156.0 %collective-permute-start.16 = (bf16[896,1024]{1,0:T(8,128)(2,1)}, bf16[896,1024]{1,0:T(8,128)(2,1)}, u32[]{:S(2)}, u32[]{:S(2)}) collective-permute-start(bf16[896,1024]{1,0:T(8,128)(2,1)} %get-tuple-element.66), channel_id=1, source_target_pairs={{0,1},{1,2},{2,3},{3,4},{4,5},{5,6},{6,7},{8,9},{9,10},{10,11},{11... | collective-permute-start | bytes 5505032 | tf_op jit(solution)/shard_map/ppermute | solution.py:16
  192.0 120.7 %collective-permute-start.17 = (bf16[896,1024]{1,0:T(8,128)(2,1)}, bf16[896,1024]{1,0:T(8,128)(2,1)}, u32[]{:S(2)}, u32[]{:S(2)}) collective-permute-start(bf16[896,1024]{1,0:T(8,128)(2,1)} %get-tuple-element.65), channel_id=1, source_target_pairs={{1,0},{2,1},{3,2},{4,3},{5,4},{6,5},{7,6},{9,8},{10,9},{11,10},{12... | collective-permute-start | bytes 5505032 | tf_op jit(solution)/shard_map/ppermute | solution.py:16
  193.3 82.1 %collective-permute-start.5 = (bf16[384,512]{1,0:T(8,128)(2,1)}, bf16[384,512]{1,0:T(8,128)(2,1)}, u32[]{:S(2)}, u32[]{:S(2)}) collective-permute-start(bf16[384,512]{1,0:T(8,128)(2,1)} %get-tuple-element.59), channel_id=1, source_target_pairs={{0,6},{1,7},{2,0},{3,1},{4,2},{5,3},{6,4},{7,5},{8,14},{9,15},{10,... | collective-permute-start | bytes 1179656 | tf_op jit(solution)/shard_map/ppermute | solution.py:21
  288.9 26.2 %collective-permute-start.9 = (bf16[384,512]{1,0:T(8,128)(2,1)S(1)}, bf16[384,512]{1,0:T(8,128)(2,1)S(1)}, u32[]{:S(2)}, u32[]{:S(2)}) collective-permute-start(bf16[384,512]{1,0:T(8,128)(2,1)S(1)} %subtract_convert_fusion), channel_id=1, source_target_pairs={{0,1},{1,2},{2,3},{3,4},{4,5},{5,6},{6,7},{7,0},{8,9},{9,10},{10,1... | collective-permute-start | bytes 1179656 | tf_op jit(solution)/shard_map/ppermute | solution.py:21
  289.0 26.2 %collective-permute-start.10 = (bf16[384,512]{1,0:T(8,128)(2,1)S(1)}, bf16[384,512]{1,0:T(8,128)(2,1)S(1)}, u32[]{:S(2)}, u32[]{:S(2)}) collective-permute-start(bf16[384,512]{1,0:T(8,128)(2,1)S(1)} %subtract_convert_fusion), channel_id=1, source_target_pairs={{0,2},{1,3},{2,4},{3,5},{4,6},{5,7},{6,0},{7,1},{8,10},{9,11},{10,... | collective-permute-start | bytes 1179656 | tf_op jit(solution)/shard_map/ppermute | solution.py:21
  304.3 32.6 %collective-permute-start.11 = (bf16[384,512]{1,0:T(8,128)(2,1)S(1)}, bf16[384,512]{1,0:T(8,128)(2,1)S(1)}, u32[]{:S(2)}, u32[]{:S(2)}) collective-permute-start(bf16[384,512]{1,0:T(8,128)(2,1)S(1)} %subtract_convert_fusion), channel_id=1, source_target_pairs={{0,3},{1,4},{2,5},{3,6},{4,7},{5,0},{6,1},{7,2},{8,11},{9,12},{10,... | collective-permute-start | bytes 1179656 | tf_op jit(solution)/shard_map/ppermute | solution.py:21
  312.7 32.1 %collective-permute-start.12 = (bf16[384,512]{1,0:T(8,128)(2,1)S(1)}, bf16[384,512]{1,0:T(8,128)(2,1)S(1)}, u32[]{:S(2)}, u32[]{:S(2)}) collective-permute-start(bf16[384,512]{1,0:T(8,128)(2,1)S(1)} %subtract_convert_fusion), channel_id=1, source_target_pairs={{0,4},{1,5},{2,6},{3,7},{4,0},{5,1},{6,2},{7,3},{8,12},{9,13},{10,... | collective-permute-start | bytes 1179656 | tf_op jit(solution)/shard_map/ppermute | solution.py:21
  312.7 32.1 %collective-permute-start.13 = (bf16[384,512]{1,0:T(8,128)(2,1)S(1)}, bf16[384,512]{1,0:T(8,128)(2,1)S(1)}, u32[]{:S(2)}, u32[]{:S(2)}) collective-permute-start(bf16[384,512]{1,0:T(8,128)(2,1)S(1)} %subtract_convert_fusion), channel_id=1, source_target_pairs={{0,5},{1,6},{2,7},{3,0},{4,1},{5,2},{6,3},{7,4},{8,13},{9,14},{10,... | collective-permute-start | bytes 1179656 | tf_op jit(solution)/shard_map/ppermute | solution.py:21
  315.1 32.5 %collective-permute-start.14 = (bf16[384,512]{1,0:T(8,128)(2,1)S(1)}, bf16[384,512]{1,0:T(8,128)(2,1)S(1)}, u32[]{:S(2)}, u32[]{:S(2)}) collective-permute-start(bf16[384,512]{1,0:T(8,128)(2,1)S(1)} %subtract_convert_fusion), channel_id=1, source_target_pairs={{0,6},{1,7},{2,0},{3,1},{4,2},{5,3},{6,4},{7,5},{8,14},{9,15},{10,... | collective-permute-start | bytes 1179656 | tf_op jit(solution)/shard_map/ppermute | solution.py:21
  315.2 38.5 %collective-permute-start.15 = (bf16[384,512]{1,0:T(8,128)(2,1)S(1)}, bf16[384,512]{1,0:T(8,128)(2,1)}, u32[]{:S(2)}, u32[]{:S(2)}) collective-permute-start(bf16[384,512]{1,0:T(8,128)(2,1)S(1)} %subtract_convert_fusion), channel_id=1, source_target_pairs={{0,7},{1,0},{2,1},{3,2},{4,3},{5,4},{6,5},{7,6},{8,15},{9,8},{10,9... | collective-permute-start | bytes 1179656 | tf_op jit(solution)/shard_map/ppermute | solution.py:21
  500.6 17.4 %collective-permute-start.20 = (bf16[128,1024]{1,0:T(8,128)(2,1)S(1)}, bf16[128,1024]{1,0:T(8,128)(2,1)S(1)}, u32[]{:S(2)}, u32[]{:S(2)}) collective-permute-start(bf16[128,1024]{1,0:T(8,128)(2,1)S(1)} %get-tuple-element.73), channel_id=1, source_target_pairs={{0,5},{1,6},{2,7},{3,0},{4,1},{5,2},{6,3},{7,4},{8,13},{9,14},{10,... | collective-permute-start | bytes 786440 | tf_op jit(solution)/shard_map/ppermute | solution.py:21
  507.8 37.6 %collective-permute-start.21 = (bf16[128,1024]{1,0:T(8,128)(2,1)S(1)}, bf16[128,1024]{1,0:T(8,128)(2,1)S(1)}, u32[]{:S(2)}, u32[]{:S(2)}) collective-permute-start(bf16[128,1024]{1,0:T(8,128)(2,1)S(1)} %get-tuple-element.72), channel_id=1, source_target_pairs={{0,4},{1,5},{2,6},{3,7},{4,0},{5,1},{6,2},{7,3},{8,12},{9,13},{10,... | collective-permute-start | bytes 786440 | tf_op jit(solution)/shard_map/ppermute | solution.py:21
  510.9 35.1 %collective-permute-start.22 = (bf16[128,1024]{1,0:T(8,128)(2,1)S(1)}, bf16[128,1024]{1,0:T(8,128)(2,1)S(1)}, u32[]{:S(2)}, u32[]{:S(2)}) collective-permute-start(bf16[128,1024]{1,0:T(8,128)(2,1)S(1)} %get-tuple-element.71), channel_id=1, source_target_pairs={{0,3},{1,4},{2,5},{3,6},{4,7},{5,0},{6,1},{7,2},{8,11},{9,12},{10,... | collective-permute-start | bytes 786440 | tf_op jit(solution)/shard_map/ppermute | solution.py:21
  510.9 35.1 %collective-permute-start.23 = (bf16[128,1024]{1,0:T(8,128)(2,1)S(1)}, bf16[128,1024]{1,0:T(8,128)(2,1)S(1)}, u32[]{:S(2)}, u32[]{:S(2)}) collective-permute-start(bf16[128,1024]{1,0:T(8,128)(2,1)S(1)} %get-tuple-element.70), channel_id=1, source_target_pairs={{0,2},{1,3},{2,4},{3,5},{4,6},{5,7},{6,0},{7,1},{8,10},{9,11},{10,... | collective-permute-start | bytes 786440 | tf_op jit(solution)/shard_map/ppermute | solution.py:21
  512.9 33.2 %collective-permute-start.24 = (bf16[128,1024]{1,0:T(8,128)(2,1)S(1)}, bf16[128,1024]{1,0:T(8,128)(2,1)S(1)}, u32[]{:S(2)}, u32[]{:S(2)}) collective-permute-start(bf16[128,1024]{1,0:T(8,128)(2,1)S(1)} %get-tuple-element.69), channel_id=1, source_target_pairs={{0,1},{1,2},{2,3},{3,4},{4,5},{5,6},{6,7},{7,0},{8,9},{9,10},{10,1... | collective-permute-start | bytes 786440 | tf_op jit(solution)/shard_map/ppermute | solution.py:21
  (28 other events, 657.9 us)
Sparse Core Ops, SparseCore 0:
  9.5 232.5 all-gather.2
  409.3 77.1 all-gather.4
